TPU v7x, 32 devices: a whole 2x2x4 slice. The times are simulated.
32 devices in a mesh: gx: 4 (over z), gy: 8 (over y, x, core).
Axes of the slice: x: 2, y: 2, z: 4, core: 2. Of those that a mesh axis runs over, the one named last changes fastest.
Arguments:
- observed: bfloat16 [1024, 1024, 128], P('gx', 'gy'), may hold values from -6 to 6
- confidence: bfloat16 [1024, 1024, 128], P('gx', 'gy'), may hold values from 0.1 to 13
- iterate: float32 [1024, 1024, 128], P('gx', 'gy'), may hold values from -24 to 24
- kernel_bank: float32 [3, 64], replicated, may hold values from 0.02 to 1
- tap_index: int32 [3, 33], replicated, may hold values from 0 to 63
- offsets: int32 [3], replicated, may hold values from -4 to 4
- basis_x: bfloat16 [1024, 1024], P('gx'), may hold values from -0.1875 to 0.1875
- basis_y: bfloat16 [1024, 1024], P('gy'), may hold values from -0.1875 to 0.1875
- basis_z: bfloat16 [128, 128], replicated, may hold values from -0.5 to 0.5
- eigen_x: float32 [1024], P('gx'), may hold values from 0.1 to 1
- eigen_y: float32 [1024], replicated, may hold values from 0.1 to 1
- eigen_z: float32 [128], replicated, may hold values from 0.1 to 1
Outputs:
- updated: float32 [1024, 1024, 128], P('gx', 'gy')
- residual: float32 [1024, 1024, 128], P('gx', 'gy')
All inputs are finite; a program needn't handle non-finite values.
Results may differ from a plain program's by a relative error of at most 0.0028.
Values may be sent and summed in bfloat16 or wider, within the bound.
A program may use at most 256 MiB of HBM per device.

v0:
```python
import jax
import jax.numpy as jnp
from jax import lax
from jax.sharding import PartitionSpec as P

HALF = 16
SHIFT = 4


highest = lax.Precision.HIGHEST
tikhonov = 0.002


def with_halo(block, sides, width):
    for axis, dim in sides:
        count = lax.axis_size(axis)
        forward = [(i, i + 1) for i in range(count - 1)]
        backward = [(target, source) for source, target in forward]
        low = lax.ppermute(
            lax.slice_in_dim(block, block.shape[dim] - width, None, axis=dim), axis, forward
        )
        high = lax.ppermute(lax.slice_in_dim(block, 0, width, axis=dim), axis, backward)
        block = jnp.concatenate([low, block, high], axis=dim)
    return block


def kernels_of(kernel_bank, tap_index):
    entries = jnp.arange(kernel_bank.shape[1], dtype=jnp.int32)
    chosen = tap_index[:, :, None] == entries[None, None, :]
    raw_taps = jnp.sum(jnp.where(chosen, kernel_bank[:, None, :], 0.0), axis=2)
    return raw_taps / jnp.sum(raw_taps, axis=1, keepdims=True)


def band_matrix(kernel, offset, out_count, in_count, margin):
    center = (kernel.shape[0] - 1) // 2
    row_pos = lax.broadcasted_iota(jnp.int32, (out_count, in_count), 0)
    col_pos = lax.broadcasted_iota(jnp.int32, (out_count, in_count), 1)
    position = col_pos - row_pos - margin + center - offset
    tap_ids = jnp.arange(kernel.shape[0], dtype=jnp.int32)
    chosen = position[None, :, :] == tap_ids[:, None, None]
    return jnp.sum(jnp.where(chosen, kernel[:, None, None], 0.0), axis=0)


def apply_blur(source, kernels, offsets):
    rim_width = HALF + SHIFT
    block_x, block_y, depth = source.shape
    z_matrix = band_matrix(kernels[2], offsets[2], depth, depth, 0)
    along_z = jnp.einsum("xyc,zc->xyz", source, z_matrix, precision=highest)
    x_matrix = band_matrix(kernels[0], offsets[0], block_x, block_x + 2 * rim_width, rim_width)
    y_matrix = band_matrix(kernels[1], offsets[1], block_y, block_y + 2 * rim_width, rim_width)
    extended = with_halo(along_z.astype(jnp.bfloat16), (("gx", 0), ("gy", 1)), HALF + SHIFT).astype(
        along_z.dtype
    )
    along_x = jnp.einsum("ic,cyz->iyz", x_matrix, extended, precision=highest)
    return jnp.einsum("jc,xcz->xjz", y_matrix, along_x, precision=highest)


def along_first(source, product):
    pencil = lax.all_to_all(source, "gx", split_axis=1, concat_axis=0, tiled=True)
    columns = pencil.reshape(pencil.shape[0], -1)
    transformed = product(columns).astype(jnp.bfloat16).reshape(pencil.shape)
    return lax.all_to_all(transformed, "gx", split_axis=0, concat_axis=1, tiled=True)


def shards(
    observed,
    confidence,
    iterate,
    kernel_bank,
    tap_index,
    offsets,
    basis_x,
    basis_y,
    basis_z,
    eigen_x,
    eigen_y,
    eigen_z,
):
    kernels = kernels_of(kernel_bank, tap_index)
    adjoint_kernels = kernels[:, ::-1]
    weights = confidence.astype(jnp.float32)
    misfit = observed.astype(jnp.float32) - apply_blur(iterate, kernels, offsets)
    gradient = apply_blur(weights * misfit, adjoint_kernels, -offsets) - tikhonov * iterate
    full_x = lax.all_gather(basis_x, "gx", axis=0, tiled=True)
    full_y = lax.all_gather(basis_y, "gy", axis=0, tiled=True)

    def x_into(columns):
        return lax.dot_general(
            full_x, columns, (((0,), (0,)), ((), ())), preferred_element_type=jnp.float32
        )

    def x_back(columns):
        return jnp.dot(full_x, columns, preferred_element_type=jnp.float32)

    gradient_b = gradient.astype(jnp.bfloat16)
    section_one = jnp.einsum(
        "xyz,zk->xyk", gradient_b, basis_z, preferred_element_type=jnp.float32
    ).astype(jnp.bfloat16)
    section_two = along_first(section_one, x_into)
    y_pencil = lax.all_to_all(section_two, "gy", split_axis=0, concat_axis=1, tiled=True)
    share_rows = y_pencil.shape[0]
    eigen_share = lax.dynamic_slice_in_dim(eigen_x, lax.axis_index("gy") * share_rows, share_rows)
    inverse = 1.0 / (
        eigen_share[:, None, None] * eigen_y[None, :, None] * eigen_z[None, None, :] + tikhonov
    )
    section_four = (
        jnp.einsum("ayz,yk->akz", y_pencil, full_y, preferred_element_type=jnp.float32) * inverse
    ).astype(jnp.bfloat16)
    section_five = jnp.einsum(
        "akz,jk->ajz", section_four, full_y, preferred_element_type=jnp.float32
    ).astype(jnp.bfloat16)
    section_five = lax.all_to_all(section_five, "gy", split_axis=1, concat_axis=0, tiled=True)
    section_six = along_first(section_five, x_back)
    direction = jnp.einsum("xyk,zk->xyz", section_six, basis_z, preferred_element_type=jnp.float32)
    local_descent = jnp.sum(gradient * direction)
    descent = lax.psum(local_descent, ("gx", "gy"))
    blurred = apply_blur(direction, kernels, offsets)
    data_sum, norm_sum = lax.psum(
        (jnp.sum(weights * blurred * blurred), jnp.sum(direction * direction)), ("gx", "gy")
    )
    energy = data_sum + tikhonov * norm_sum
    step_size = descent / energy
    return (iterate + step_size * direction, misfit - step_size * blurred)


def solution(mesh):
    return jax.shard_map(
        shards,
        mesh=mesh,
        in_specs=(
            P("gx", "gy", None),
            P("gx", "gy", None),
            P("gx", "gy", None),
            P(),
            P(),
            P(),
            P("gx", None),
            P("gy", None),
            P(),
            P("gx"),
            P(),
            P(),
        ),
        out_specs=(P("gx", "gy", None), P("gx", "gy", None)),
        check_vma=False,
    )
```

profile of v0, /device:TPU:0, one launch (start us, length us, event | category | flops | bytes accessed | tf_op | source)
XLA Modules:
  0.0 1968.8 jit_solution(5381071775387869548)
XLA Ops:
  93.5 25.4 %pad_maximum_fusion = bf16[296,168,128]{2,1,0:T(8,128)(2,1)S(1)} fusion(bf16[296,20,128]{2,1,0:T(8,128)(2,1)S(1)} %copy.149, bf16[20,128,128]{2,1,0:T(8,128)(2,1)S(1)} %collective-permute-done.1, bf16[256,128,128]{2,1,0:T(8,128)(2,1)} %copy-done.3, bf16[20,128,128]{2,1,0:T(8,128)(2,1)S(1)} %collective-permute-done, bf16[296,20,128]{2,1,0:T(8,128)(2,1)S(1)} %copy.148), kind=kLoop, calls=%fused_computation.19 | loop fusion | flops 63651840 | bytes 25460736 | tf_op jit(solution)/shard_map/concatenate | solution.py:23
  119.0 20.9 %fusion.14 = f32[256,168,128]{2,0,1:T(8,128)} fusion(bf16[296,168,128]{2,1,0:T(8,128)(2,1)S(1)} %pad_maximum_fusion, f32[256,296]{0,1:T(8,128)S(1)} %select_reduce_fusion), kind=kOutput, calls=%fused_computation.26 | convolution fusion | flops 19553845248 | bytes 35053568 | tf_op jit(solution)/shard_map/ic,cyz->iyz/dot_general | solution.py:54
  139.9 77.2 %fusion.4 = f32[256,128,128]{2,1,0:T(8,128)S(1)} fusion(f32[256,168,128]{2,0,1:T(8,128)} %fusion.14, f32[128,168]{0,1:T(8,128)S(1)} %select_reduce_fusion.3), kind=kOutput, calls=%fused_computation.5 | convolution fusion | flops 8455716864 | bytes 38883328 | tf_op jit(solution)/shard_map/jc,xcz->xjz/dot_general | solution.py:55
  217.2 31.8 %fusion.35 = bf16[256,128,128]{2,1,0:T(8,128)(2,1)} fusion(bf16[256,128,128]{1,2,0:T(8,128)(2,1)S(1)} %bitcast.127, f32[256,128,128]{2,1,0:T(8,128)S(1)} %fusion.4, bf16[256,128,128]{1,2,0:T(8,128)(2,1)} %copy.145, f32[128,128]{1,0:T(8,128)S(1)} %select_reduce_fusion.4), kind=kOutput, calls=%fused_computation.45 | convolution fusion | flops 6463422464 | bytes 42008576 | tf_op jit(solution)/shard_map/xyc,zc->xyz/dot_general | solution.py:48
  285.3 17.6 copy.182
  309.1 26.9 %pad_maximum_fusion.1 = bf16[296,168,128]{2,1,0:T(8,128)(2,1)} fusion(bf16[296,20,128]{2,1,0:T(8,128)(2,1)S(1)} %copy.156, bf16[20,128,128]{2,1,0:T(8,128)(2,1)S(1)} %collective-permute-done.5, bf16[256,128,128]{2,1,0:T(8,128)(2,1)} %fusion.35, bf16[20,128,128]{2,1,0:T(8,128)(2,1)S(1)} %collective-permute-done.4, bf16[296,20,128]{2,1,0:T(8,128)(2,1)S(1)} %copy.155), kind=kLoop, calls=%fused_computation.20 | loop fusion | flops 63651840 | bytes 25460736 | tf_op jit(solution)/shard_map/concatenate | solution.py:23
  336.0 27.2 %fusion.12 = f32[256,168,128]{2,0,1:T(8,128)} fusion(bf16[296,168,128]{2,1,0:T(8,128)(2,1)} %pad_maximum_fusion.1, f32[256,296]{0,1:T(8,128)S(1)} %select_reduce_fusion.1), kind=kOutput, calls=%fused_computation.24 | convolution fusion | flops 19553845248 | bytes 35053568 | tf_op jit(solution)/shard_map/ic,cyz->iyz/dot_general | solution.py:54
  363.3 68.3 %bitcast_subtract_fusion = f32[256,128,128]{1,2,0:T(8,128)} fusion(f32[256,128,128]{1,2,0:T(8,128)S(1)} %bitcast.125, f32[256,168,128]{2,0,1:T(8,128)} %fusion.12, f32[128,168]{0,1:T(8,128)S(1)} %select_reduce_fusion.2), kind=kOutput, calls=%fused_computation.14 | convolution fusion | flops 8464105472 | bytes 55660544 | tf_op jit(solution)/shard_map/jc,xcz->xjz/dot_general | solution.py:55
  461.5 216.4 %all-to-all-done = bf16[256,128,128]{2,0,1:T(8,128)(2,1)} async-done(((bf16[256,128,128]{2,0,1:T(8,128)(2,1)}), bf16[256,128,128]{2,0,1:T(8,128)(2,1)}, u32[]{:S(2)}, u32[]{:S(2)}) %all-to-all-start) | async-done | bytes 8388640 | tf_op jit(solution)/shard_map/all_to_all | solution.py:59
  690.1 20.1 %fusion.26 = bf16[4096,1024]{1,0:T(8,128)(2,1)} fusion(bf16[1024,1024]{1,0:T(8,128)(2,1)} %all-gather.3.cloned.1.call-done, bf16[128,8,32,128]{3,2,1,0:T(8,128)(2,1)} %bitcast.138), kind=kOutput, calls=%fused_computation.42 | convolution fusion | flops 8594128896 | bytes 18874368 | tf_op jit(solution)/shard_map/dot_general | solution.py:88
  722.7 192.4 %all_to_all.102 = bf16[1024,32,128]{2,1,0:T(8,128)(2,1)} all-to-all(bf16[1024,32,128]{2,1,0:T(8,128)(2,1)} %copy.163), channel_id=1, replica_groups=mesh['gx'=4,'gy'=8] {'gx'}, dimensions={0} | all-to-all | bytes 16777216 | tf_op jit(solution)/shard_map/all_to_all | solution.py:62
  936.9 101.8 %all-to-all-done.2 = bf16[256,128,128]{2,1,0:T(8,128)(2,1)} async-done(((bf16[256,128,128]{2,1,0:T(8,128)(2,1)}), bf16[256,128,128]{2,1,0:T(8,128)(2,1)}, u32[]{:S(2)}, u32[]{:S(2)}) %all-to-all-start.2) | async-done | bytes 8388640 | tf_op jit(solution)/shard_map/all_to_all | solution.py:100
  1049.2 25.6 %convert_bitcast_fusion = bf16[32,1024,128]{1,2,0:T(8,128)(2,1)} fusion(bf16[32,1024,128]{2,1,0:T(8,128)(2,1)} %bitcast.137, f32[128]{0:T(128)S(1)} %copy-done.15, f32[32,1024]{1,0:T(8,128)S(1)} %broadcast_multiply_fusion, bf16[1024,1024]{1,0:T(8,128)(2,1)} %all-gather.5.cloned.1.call-done), kind=kOutput, calls=%fused_computation.38 | convolution fusion | flops 17205035008 | bytes 19005952 | tf_op jit(solution)/shard_map/akz,jk->ajz/dot_general | solution.py:109
  1087.3 99.9 %all_to_all.103 = bf16[32,1024,128]{2,0,1:T(8,128)(2,1)} all-to-all(bf16[32,1024,128]{2,0,1:T(8,128)(2,1)} %copy.167), channel_id=1, replica_groups=mesh['gx'=4,'gy'=8] {'gy'}, dimensions={1} | all-to-all | bytes 16777216 | tf_op jit(solution)/shard_map/all_to_all | solution.py:112
  1209.3 190.3 %all_to_all.104 = bf16[256,128,128]{2,0,1:T(8,128)(2,1)} all-to-all(bf16[256,128,128]{2,0,1:T(8,128)(2,1)} %copy.170), channel_id=1, replica_groups=mesh['gx'=4,'gy'=8] {'gx'}, dimensions={1} | all-to-all | bytes 16777216 | tf_op jit(solution)/shard_map/all_to_all | solution.py:59
  1411.8 21.1 %fusion.29 = bf16[4096,1024]{1,0:T(8,128)(2,1)} fusion(bf16[1024,1024]{1,0:T(8,128)(2,1)S(1)} %copy-done.13, bf16[128,8,32,128]{3,2,1,0:T(8,128)(2,1)} %bitcast.139), kind=kOutput, calls=%fused_computation.43 | convolution fusion | flops 8594128896 | bytes 18874368 | tf_op jit(solution)/shard_map/dot_general | solution.py:93
  1445.4 190.0 %all_to_all.105 = bf16[1024,32,128]{2,1,0:T(8,128)(2,1)} all-to-all(bf16[1024,32,128]{2,1,0:T(8,128)(2,1)} %copy.172), channel_id=1, replica_groups=mesh['gx'=4,'gy'=8] {'gx'}, dimensions={0} | all-to-all | bytes 16777216 | tf_op jit(solution)/shard_map/all_to_all | solution.py:62
  1695.9 17.6 copy.174
  1729.5 25.6 %pad_maximum_fusion.2 = bf16[296,168,128]{2,1,0:T(8,128)(2,1)S(1)} fusion(bf16[296,20,128]{2,1,0:T(8,128)(2,1)S(1)} %copy.178, bf16[20,128,128]{2,1,0:T(8,128)(2,1)S(1)} %collective-permute-done.9, bf16[256,128,128]{2,1,0:T(8,128)(2,1)} %copy-done.4, bf16[20,128,128]{2,1,0:T(8,128)(2,1)S(1)} %collective-permute-done.8, bf16[296,20,128]{2,1,0:T(8,128)(2,1)S(1)} %copy.177), kind=kLoop, calls=%fused_computation.21 | loop fusion | flops 63651840 | bytes 25460736 | tf_op jit(solution)/shard_map/concatenate | solution.py:23
  1755.1 21.0 %fusion.10 = f32[256,168,128]{2,0,1:T(8,128)} fusion(bf16[296,168,128]{2,1,0:T(8,128)(2,1)S(1)} %pad_maximum_fusion.2, f32[256,296]{0,1:T(8,128)S(1)} %copy-done.6), kind=kOutput, calls=%fused_computation.22 | convolution fusion | flops 19553845248 | bytes 35053568 | tf_op jit(solution)/shard_map/ic,cyz->iyz/dot_general | solution.py:54
  1776.2 68.6 %fusion.7 = (f32[]{:T(128)}, f32[256,128,128]{2,1,0:T(8,128)}) fusion(bf16[256,128,128]{1,2,0:T(8,128)(2,1)S(1)} %bitcast.129, f32[128,168]{0,1:T(8,128)S(1)} %copy-done.8, f32[256,168,128]{2,0,1:T(8,128)} %fusion.10), kind=kOutput, calls=%fused_computation.9 | convolution fusion | flops 8472494080 | bytes 47271940 | tf_op jit(solution)/shard_map/jc,xcz->xjz/dot_general | solution.py:55
  1844.8 41.9 %all-reduce = (f32[]{:T(128)}, f32[]{:T(128)}, f32[]{:T(128)}) all-reduce(f32[]{:T(128)} %multiply_reduce_fusion.1, f32[]{:T(128)} %get-tuple-element.43, f32[]{:T(128)} %get-tuple-element.45), channel_id=1, replica_groups=mesh['gx'=4,'gy'=8] {'gx','gy'}, use_global_device_ids=true, to_apply=%region_9.10 | all-reduce | flops 3 | bytes 24 | tf_op jit(solution)/shard_map/psum | solution.py:116
  1888.5 37.5 %fusion.8 = (f32[256,128,128]{1,2,0:T(8,128)}, f32[256,128,128]{1,2,0:T(8,128)}) fusion(f32[256,128,128]{2,1,0:T(8,128)} %get-tuple-element.44, f32[256,128,128]{2,1,0:T(8,128)} %copy-done.2, bf16[256,128,128]{1,2,0:T(8,128)(2,1)} %copy.145, f32[]{:T(128)S(6)} %div.21, f32[256,128,128]{1,2,0:T(8,128)} %copy.182, f32[256,128,128]{1,2,0:T(8,128)} %copy.174), kind=kLoop, calls=%fused_computation.11 | loop fusion | flops 25165824 | bytes 109051904 | tf_op jit(solution)/shard_map/sub | solution.py:123
  1926.0 17.4 copy.183
  (143 shorter events, 367.6 us)
Async XLA Ops:
  8.0 423.6 %copy-start = (bf16[128,128]{1,0:T(8,128)(2,1)S(1)}, bf16[128,128]{1,0:T(8,128)(2,1)}, u32[]{:S(2)}) copy-start(bf16[128,128]{1,0:T(8,128)(2,1)} %param.20) | copy-start | bytes 98308
  27.5 18.9 collective-permute-start
  32.5 18.1 collective-permute-start.1
  56.5 33.5 %collective-permute-start.2 = (bf16[296,20,128]{2,0,1:T(8,128)(2,1)S(1)}, bf16[296,20,128]{2,0,1:T(8,128)(2,1)}, u32[]{:S(2)}, u32[]{:S(2)}) collective-permute-start(bf16[296,20,128]{2,0,1:T(8,128)(2,1)S(1)} %copy.146), channel_id=1, source_target_pairs={{0,1},{1,2},{2,3},{3,4},{4,5},{5,6},{6,7},{8,9},{9,10},{10,11},{11... | collective-permute-start | bytes 4546568 | tf_op jit(solution)/shard_map/ppermute | solution.py:19
  60.3 31.5 %collective-permute-start.3 = (bf16[296,20,128]{2,0,1:T(8,128)(2,1)}, bf16[296,20,128]{2,0,1:T(8,128)(2,1)}, u32[]{:S(2)}, u32[]{:S(2)}) collective-permute-start(bf16[296,20,128]{2,0,1:T(8,128)(2,1)} %copy.147), channel_id=1, source_target_pairs={{1,0},{2,1},{3,2},{4,3},{5,4},{6,5},{7,6},{9,8},{10,9},{11,10},{12... | collective-permute-start | bytes 4546568 | tf_op jit(solution)/shard_map/ppermute | solution.py:22
  89.0 50.9 %copy-start.7 = (f32[128,168]{0,1:T(8,128)}, f32[128,168]{0,1:T(8,128)S(1)}, u32[]{:S(2)}) copy-start(f32[128,168]{0,1:T(8,128)S(1)} %select_reduce_fusion.3) | copy-start | bytes 258052
  118.9 98.2 %slice-start.4 = ((s8[8388608]{0:T(1024)(128)(4,1)}), s8[4194304]{0:T(1024)(128)(4,1)S(1)}, s32[]{:S(2)}) async-start(s8[8388608]{0:T(1024)(128)(4,1)} %bitcast.126), calls=%async_computation.12 | async-start | bytes 8388608
  139.9 77.3 %slice-start.5 = ((s8[8388608]{0:T(1024)(128)(4,1)}), s8[4194304]{0:T(1024)(128)(4,1)S(1)}, s32[]{:S(2)}) async-start(s8[8388608]{0:T(1024)(128)(4,1)} %bitcast.126), calls=%async_computation.13 | async-start | bytes 8388608
  217.2 31.8 %copy-start.2 = (f32[256,128,128]{2,1,0:T(8,128)}, f32[256,128,128]{2,1,0:T(8,128)S(1)}, u32[]{:S(2)}) copy-start(f32[256,128,128]{2,1,0:T(8,128)S(1)} %fusion.4) | copy-start | bytes 50331652
  250.4 16.5 collective-permute-start.4
  253.9 17.8 collective-permute-start.5
  278.0 27.7 %collective-permute-start.6 = (bf16[296,20,128]{2,0,1:T(8,128)(2,1)S(1)}, bf16[296,20,128]{2,0,1:T(8,128)(2,1)}, u32[]{:S(2)}, u32[]{:S(2)}) collective-permute-start(bf16[296,20,128]{2,0,1:T(8,128)(2,1)S(1)} %copy.153), channel_id=1, source_target_pairs={{0,1},{1,2},{2,3},{3,4},{4,5},{5,6},{6,7},{8,9},{9,10},{10,11},{11... | collective-permute-start | bytes 4546568 | tf_op jit(solution)/shard_map/ppermute | solution.py:19
  284.0 23.4 %collective-permute-start.7 = (bf16[296,20,128]{2,0,1:T(8,128)(2,1)}, bf16[296,20,128]{2,0,1:T(8,128)(2,1)}, u32[]{:S(2)}, u32[]{:S(2)}) collective-permute-start(bf16[296,20,128]{2,0,1:T(8,128)(2,1)} %copy.154), channel_id=1, source_target_pairs={{1,0},{2,1},{3,2},{4,3},{5,4},{6,5},{7,6},{9,8},{10,9},{11,10},{12... | collective-permute-start | bytes 4546568 | tf_op jit(solution)/shard_map/ppermute | solution.py:22
  309.1 54.2 %slice-start = ((s8[16777216]{0:T(1024)(128)(4,1)}), s8[4194304]{0:T(1024)(128)(4,1)S(1)}, s32[]{:S(2)}) async-start(s8[16777216]{0:T(1024)(128)(4,1)} %bitcast.124), calls=%async_computation.8 | async-start | bytes 8388608
  309.1 54.1 %slice-start.1 = ((s8[16777216]{0:T(1024)(128)(4,1)}), s8[4194304]{0:T(1024)(128)(4,1)S(1)}, s32[]{:S(2)}) async-start(s8[16777216]{0:T(1024)(128)(4,1)} %bitcast.124), calls=%async_computation.9 | async-start | bytes 8388608
  455.1 222.8 %all-to-all-start = ((bf16[256,128,128]{2,0,1:T(8,128)(2,1)}), bf16[256,128,128]{2,0,1:T(8,128)(2,1)}, u32[]{:S(2)}, u32[]{:S(2)}) async-start(bf16[256,128,128]{2,0,1:T(8,128)(2,1)} %copy.161), calls=%async_computation | async-start | bytes 16777216 | tf_op jit(solution)/shard_map/all_to_all | solution.py:59
  460.8 229.3 %all-gather.3.cloned.1.call-start = ((), (), s32[]{:S(2)}) async-start(), calls=%async_computation.6 | async-start | bytes 2621440 | tf_op jit(solution)/shard_map/all_gather | solution.py:84
  924.5 114.3 %all-to-all-start.2 = ((bf16[256,128,128]{2,1,0:T(8,128)(2,1)}), bf16[256,128,128]{2,1,0:T(8,128)(2,1)}, u32[]{:S(2)}, u32[]{:S(2)}) async-start(bf16[256,128,128]{2,1,0:T(8,128)(2,1)} %bitcast.131), calls=%async_computation.2 | async-start | bytes 16777216 | tf_op jit(solution)/shard_map/all_to_all | solution.py:100
  936.1 113.1 %all-gather.5.cloned.1.call-start = ((), (), s32[]{:S(2)}) async-start(), calls=%async_computation.7 | async-start | bytes 2359296 | tf_op jit(solution)/shard_map/all_gather | solution.py:85
  1666.1 14.6 collective-permute-start.8
  1668.3 16.6 collective-permute-start.9
  1690.8 35.4 %collective-permute-start.10 = (bf16[296,20,128]{2,0,1:T(8,128)(2,1)S(1)}, bf16[296,20,128]{2,0,1:T(8,128)(2,1)}, u32[]{:S(2)}, u32[]{:S(2)}) collective-permute-start(bf16[296,20,128]{2,0,1:T(8,128)(2,1)S(1)} %copy.175), channel_id=1, source_target_pairs={{0,1},{1,2},{2,3},{3,4},{4,5},{5,6},{6,7},{8,9},{9,10},{10,11},{11... | collective-permute-start | bytes 4546568 | tf_op jit(solution)/shard_map/ppermute | solution.py:19
  1694.6 33.2 %collective-permute-start.11 = (bf16[296,20,128]{2,0,1:T(8,128)(2,1)}, bf16[296,20,128]{2,0,1:T(8,128)(2,1)}, u32[]{:S(2)}, u32[]{:S(2)}) collective-permute-start(bf16[296,20,128]{2,0,1:T(8,128)(2,1)} %copy.176), channel_id=1, source_target_pairs={{1,0},{2,1},{3,2},{4,3},{5,4},{6,5},{7,6},{9,8},{10,9},{11,10},{12... | collective-permute-start | bytes 4546568 | tf_op jit(solution)/shard_map/ppermute | solution.py:22
  1729.5 46.7 %slice-start.6 = ((s8[8388608]{0:T(1024)(128)(4,1)}), s8[4194304]{0:T(1024)(128)(4,1)S(1)}, s32[]{:S(2)}) async-start(s8[8388608]{0:T(1024)(128)(4,1)} %bitcast.128), calls=%async_computation.14 | async-start | bytes 8388608
  (16 other events, 319.0 us)
Sparse Core Ops, SparseCore 0:
  463.2 99.1 all-gather.2
Sparse Core Ops, SparseCore 1:
  938.5 62.5 all-gather.4
where the time goes:
time: 1980 us; the launch traced here: 1970 us
  blocking collectives  714 us (36%)
  matrix products  431 us (22%)
  waiting for transfers between devices  368 us (19%)
  local copies, waits for them, and re-layouts  238 us (12%)
  other arithmetic  154 us (8%)
  starting transfers between devices  45.6 us (2%)
    all_to_all x2, blocking collectives, along_first(): lax.all_to_all(transformed, 'gx', split_axis=0, concat_axis=1, tiled=True)  382 us
    all_to_all x1, waiting for transfers between devices, along_first(): lax.all_to_all(source, 'gx', split_axis=1, concat_axis=0, tiled=True)  216 us
    dot_general x3, matrix products, apply_blur(): return jnp.einsum('jc,xcz->xjz', y_matrix, along_x, precision=highest)  214 us
    all_to_all x1, blocking collectives, along_first(): lax.all_to_all(source, 'gx', split_axis=1, concat_axis=0, tiled=True)  190 us
    all_to_all x1, waiting for transfers between devices, shards(): lax.all_to_all(section_two, 'gy', split_axis=0, concat_axis=1, tiled=True)  102 us
    all_to_all x1, blocking collectives, shards(): lax.all_to_all(section_five, 'gy', split_axis=1, concat_axis=0, tiled=True)  99.9 us
    concatenate x3, other arithmetic, with_halo(): block = jnp.concatenate([low, block, high], axis=dim)  77.9 us
    unnamed x53, local copies, waits for them, and re-layouts  76.4 us
  transfers between devices with their start and end apart: 16, of which 8 were waited for; matrix products, arithmetic and copies ran while one was open for 6% of the time, Pallas kernels for 0%

commit v1 on v0

v1 whole, which is shorter than its diff:
```python
import jax
import jax.numpy as jnp
from jax import lax
from jax.sharding import PartitionSpec as P

HALF = 16
SHIFT = 4
CHUNKS = 2


highest = lax.Precision.HIGHEST
tikhonov = 0.002


def exchange(block, axis, dim, width):
    count = lax.axis_size(axis)
    forward = [(i, i + 1) for i in range(count - 1)]
    backward = [(target, source) for source, target in forward]
    low = lax.ppermute(
        lax.slice_in_dim(block, block.shape[dim] - width, None, axis=dim), axis, forward
    )
    high = lax.ppermute(lax.slice_in_dim(block, 0, width, axis=dim), axis, backward)
    return low, high


def kernels_of(kernel_bank, tap_index):
    entries = jnp.arange(kernel_bank.shape[1], dtype=jnp.int32)
    chosen = tap_index[:, :, None] == entries[None, None, :]
    raw_taps = jnp.sum(jnp.where(chosen, kernel_bank[:, None, :], 0.0), axis=2)
    return raw_taps / jnp.sum(raw_taps, axis=1, keepdims=True)


def band_matrix(kernel, offset, out_count, in_count, margin):
    center = (kernel.shape[0] - 1) // 2
    row_pos = lax.broadcasted_iota(jnp.int32, (out_count, in_count), 0)
    col_pos = lax.broadcasted_iota(jnp.int32, (out_count, in_count), 1)
    position = col_pos - row_pos - margin + center - offset
    tap_ids = jnp.arange(kernel.shape[0], dtype=jnp.int32)
    chosen = position[None, :, :] == tap_ids[:, None, None]
    return jnp.sum(jnp.where(chosen, kernel[:, None, None], 0.0), axis=0)


def split_dot(spec, matrix, block):
    return jnp.einsum(spec, matrix, block.astype(jnp.float32), precision=lax.Precision.HIGH)


def turned(array, axis_name, dim, sign):
    count = lax.axis_size(axis_name)
    size = array.shape[dim] // count
    mine = lax.axis_index(axis_name)
    pieces = [
        lax.dynamic_slice_in_dim(array, lax.rem(mine + sign * step + count, count) * size, size, dim)
        for step in range(count)
    ]
    return jnp.concatenate(pieces, axis=dim)


def swap(block, axis_name, split, concat, sign):
    count = lax.axis_size(axis_name)
    pieces = jnp.split(block, count, axis=split)
    arrived = [pieces[0]]
    for step in range(1, count):
        pairs = [(i, (i + sign * step) % count) for i in range(count)]
        arrived.append(lax.ppermute(pieces[step], axis_name, pairs))
    return jnp.concatenate(arrived, axis=concat)


def blur_xy(along_z, kernels, offsets):
    rim = HALF + SHIFT
    block_x, block_y, _ = along_z.shape
    x_matrix = band_matrix(kernels[0], offsets[0], block_x, block_x + 2 * rim, rim)
    y_matrix = band_matrix(kernels[1], offsets[1], block_y, block_y + 2 * rim, rim)
    low, high = exchange(along_z, "gx", 0, rim)
    extended = jnp.concatenate([low, along_z, high], axis=0)
    along_x = split_dot("ic,cyz->iyz", x_matrix, extended).astype(jnp.bfloat16)
    low, high = exchange(along_x, "gy", 1, rim)
    inner = split_dot("jc,xcz->xjz", y_matrix[:, rim:-rim], along_x)
    rims = jnp.concatenate([low, high], axis=1)
    rim_matrix = jnp.concatenate([y_matrix[:, :rim], y_matrix[:, -rim:]], axis=1)
    return inner + split_dot("jc,xcz->xjz", rim_matrix, rims)


def apply_blur(source, kernels, offsets):
    depth = source.shape[2]
    z_matrix = band_matrix(kernels[2], offsets[2], depth, depth, 0)
    along_z = jnp.einsum("xyc,zc->xyz", source, z_matrix, precision=lax.Precision.HIGH)
    return blur_xy(along_z.astype(jnp.bfloat16), kernels, offsets)


def shards(
    observed,
    confidence,
    iterate,
    kernel_bank,
    tap_index,
    offsets,
    basis_x,
    basis_y,
    basis_z,
    eigen_x,
    eigen_y,
    eigen_z,
):
    kernels = kernels_of(kernel_bank, tap_index)
    adjoint_kernels = kernels[:, ::-1]
    weights = confidence.astype(jnp.float32)
    misfit = observed.astype(jnp.float32) - apply_blur(iterate, kernels, offsets)
    gradient = apply_blur(weights * misfit, adjoint_kernels, -offsets) - tikhonov * iterate
    full_x = lax.all_gather(basis_x, "gx", axis=0, tiled=True)
    full_y = lax.all_gather(basis_y, "gy", axis=0, tiled=True)

    gradient_b = gradient.astype(jnp.bfloat16)
    gx_size = lax.axis_size("gx")
    depth = basis_z.shape[0]
    share_z = depth // gx_size
    chunks = min(CHUNKS, share_z)
    part = share_z // chunks
    z_ahead = turned(basis_z, "gx", 1, 1).reshape(depth, gx_size, chunks, part)
    eigen_part = lax.dynamic_slice_in_dim(eigen_z, lax.axis_index("gx") * share_z, share_z)
    all_x = lax.all_gather(eigen_x, "gx", axis=0, tiled=True)
    share_x = all_x.shape[0] // lax.axis_size("gy")
    part_x = lax.dynamic_slice_in_dim(all_x, lax.axis_index("gy") * share_x, share_x)
    x_rows_behind = turned(full_x, "gx", 0, -1)
    x_ahead = turned(x_rows_behind, "gy", 1, 1)
    x_return = turned(turned(full_x, "gx", 0, 1), "gy", 1, -1)
    y_behind = turned(full_y, "gy", 0, -1)
    y_ahead = turned(full_y, "gy", 0, 1)
    found = []
    for chunk in range(chunks):
        modes = z_ahead[:, :, chunk].reshape(depth, gx_size * part)
        section_one = jnp.einsum(
            "zk,xyz->kxy", modes, gradient_b, preferred_element_type=jnp.float32
        ).astype(jnp.bfloat16)
        lines = swap(section_one, "gx", 0, 1, 1)
        section_two = jnp.einsum(
            "xj,kxy->kjy", x_ahead, lines, preferred_element_type=jnp.float32
        ).astype(jnp.bfloat16)
        lines = swap(section_two, "gy", 1, 2, 1)
        part_z = eigen_part[chunk * part : (chunk + 1) * part]
        inverse = 1.0 / (
            part_x[None, :, None] * eigen_y[None, None, :] * part_z[:, None, None] + tikhonov
        )
        section_four = (
            jnp.einsum("axy,yk->axk", lines, y_behind, preferred_element_type=jnp.float32)
            * inverse
        ).astype(jnp.bfloat16)
        section_five = jnp.einsum(
            "axk,jk->axj", section_four, y_ahead, preferred_element_type=jnp.float32
        ).astype(jnp.bfloat16)
        lines = swap(section_five, "gy", 2, 1, 1)
        section_six = jnp.einsum(
            "jx,kxy->kjy", x_return, lines, preferred_element_type=jnp.float32
        ).astype(jnp.bfloat16)
        found.append(swap(section_six, "gx", 1, 0, 1))
    section_six = jnp.concatenate(found, axis=0)
    basis_z = (
        turned(basis_z, "gx", 1, -1)
        .reshape(depth, gx_size, chunks, part)
        .transpose(0, 2, 1, 3)
        .reshape(depth, depth)
    )
    direction = jnp.einsum("kxy,zk->xyz", section_six, basis_z, preferred_element_type=jnp.float32)
    z_matrix = band_matrix(kernels[2], offsets[2], depth, depth, 0)
    z_modes = jnp.dot(z_matrix, basis_z.astype(jnp.float32), precision=highest)
    along_z = jnp.einsum(
        "kxy,zk->xyz", section_six.astype(jnp.float32), z_modes, precision=lax.Precision.HIGH
    ).astype(jnp.bfloat16)
    local_descent = jnp.sum(gradient * direction)
    descent = lax.psum(local_descent, ("gx", "gy"))
    blurred = blur_xy(along_z, kernels, offsets)
    data_sum, norm_sum = lax.psum(
        (jnp.sum(weights * blurred * blurred), jnp.sum(direction * direction)), ("gx", "gy")
    )
    energy = data_sum + tikhonov * norm_sum
    step_size = descent / energy
    return (iterate + step_size * direction, misfit - step_size * blurred)


def solution(mesh):
    return jax.shard_map(
        shards,
        mesh=mesh,
        in_specs=(
            P("gx", "gy", None),
            P("gx", "gy", None),
            P("gx", "gy", None),
            P(),
            P(),
            P(),
            P("gx", None),
            P("gy", None),
            P(),
            P("gx"),
            P(),
            P(),
        ),
        out_specs=(P("gx", "gy", None), P("gx", "gy", None)),
        check_vma=False,
    )
```

time: 1980 us -> 1160 us (0.59)
  blocking collectives: 714 us -> 56 us
  matrix products: 431 us -> 298 us
  starting transfers between devices: 45.6 us -> 157 us
  other arithmetic: 154 us -> 85.1 us
  local copies, waits for them, and re-layouts: 238 us -> 201 us
  waiting for transfers between devices: 368 us -> 341 us
    all_to_all x4 -> x0, blocking collectives: 673 us -> none  [the longest x2 382 us: along_first(): lax.all_to_all(transformed, 'gx', split_axis=0, concat_axis=1, tiled=True)]
    all_to_all x2 -> x0, waiting for transfers between devices: 318 us -> none  [the longest x1 216 us: along_first(): lax.all_to_all(source, 'gx', split_axis=1, concat_axis=0, tiled=True)]
    ppermute x12 -> x52, waiting for transfers between devices: 48.5 us -> 340 us  [the longest x40 335 us: swap(): arrived.append(lax.ppermute(pieces[step], axis_name, pairs))]
    dot_general x14 -> x22, matrix products: 431 us -> 298 us  [the longest x9 187 us: split_dot(): jnp.einsum(spec, matrix, block.astype(jnp.float32), precision=lax.Precisi...]
    ppermute x12 -> x52, starting transfers between devices: 28.2 us -> 157 us  [the longest x40 109 us: swap(): arrived.append(lax.ppermute(pieces[step], axis_name, pairs))]
    all_to_all x7 -> x0, local copies, waits for them, and re-layouts: 75.6 us -> none  [the longest x2 24.4 us: along_first(): lax.all_to_all(source, 'gx', split_axis=1, concat_axis=0, tiled=True)]
    unnamed x53 -> x163, local copies, waits for them, and re-layouts: 76.4 us -> 118 us
    concatenate x3 -> x10, other arithmetic: 77.9 us -> 36.7 us  [the longest x3 28.3 us: blur_xy(): extended = jnp.concatenate([low, along_z, high], axis=0)]
  transfers between devices with their start and end apart: 16 -> 54, of which waited for: 8 -> 20; matrix products, arithmetic and copies ran while one was open for 6% -> 33% of each run, Pallas kernels for 0% -> 0%
where the time goes in v1:
time: 1160 us
  waiting for transfers between devices  341 us (29%)
  matrix products  298 us (26%)
  local copies, waits for them, and re-layouts  201 us (17%)
  starting transfers between devices  157 us (14%)
  other arithmetic  85.1 us (7%)
  blocking collectives  56 us (5%)
  between operations  17.8 us (2%)
    ppermute x40, waiting for transfers between devices, swap(): arrived.append(lax.ppermute(pieces[step], axis_name, pairs))  335 us
    dot_general x9, matrix products, split_dot(): jnp.einsum(spec, matrix, block.astype(jnp.float32), precision=lax.Precisi...  187 us
    unnamed x163, local copies, waits for them, and re-layouts  118 us
    ppermute x40, starting transfers between devices, swap(): arrived.append(lax.ppermute(pieces[step], axis_name, pairs))  109 us
    psum x1, blocking collectives, shards(): descent = lax.psum(local_descent, ('gx', 'gy'))  45.3 us
    ppermute x6, starting transfers between devices, exchange(): lax.ppermute(lax.slice_in_dim(block, block.shape[dim] - width, None, axis...  39.9 us
    dot_general x2, matrix products, apply_blur(): jnp.einsum('xyc,zc->xyz', source, z_matrix, precision=lax.Precision.HIGH)  31.4 us
    concatenate x3, other arithmetic, blur_xy(): extended = jnp.concatenate([low, along_z, high], axis=0)  28.3 us
  transfers between devices with their start and end apart: 54, of which 20 were waited for; matrix products, arithmetic and copies ran while one was open for 33% of the time, Pallas kernels for 0%

profile of v1, /device:TPU:0, one launch (start us, length us, event | category | flops | bytes accessed | tf_op | source)
XLA Modules:
  0.0 1156.1 jit_solution(7296010660347990047)
XLA Ops:
  111.2 24.7 %fusion.11 = f32[256,128,128]{2,1,0:T(8,128)} fusion(bf16[256,128,128]{2,0,1:T(8,128)(2,1)S(1)} %convolution_convert_fusion.1, f32[128,168]{0,1:T(8,128)S(1)} %select_reduce_fusion.3), kind=kOutput, calls=%fused_computation.27 | convolution fusion | flops 3221225472 | bytes 25231360 | tf_op jit(solution)/shard_map/jc,xcz->xjz/dot_general | solution.py:44
  152.5 20.4 %fusion.13 = bf16[256,128,128]{2,1,0:T(8,128)(2,1)} fusion(f32[256,128,128]{1,2,0:T(8,128)} %bitcast_subtract_fusion.1, bf16[256,128,128]{1,2,0:T(8,128)(2,1)} %copy.125, f32[128,128]{1,0:T(8,128)S(1)} %copy-done.19), kind=kOutput, calls=%fused_computation.33 | convolution fusion | flops 3233808384 | bytes 33619968 | tf_op jit(solution)/shard_map/xyc,zc->xyz/dot_general | solution.py:86
  180.5 17.4 %copy.161 = f32[256,128,128]{1,2,0:T(8,128)} copy(f32[256,128,128]{2,1,0:T(8,128)} %param.14) | data formatting | bytes 33554432 | tf_op args[2]
  217.6 26.5 %fusion.14 = bf16[256,128,128]{2,0,1:T(8,128)(2,1)S(1)} fusion(bf16[296,128,128]{2,1,0:T(8,128)(2,1)S(1)} %pad_maximum_fusion.1, f32[256,296]{0,1:T(8,128)S(1)} %select_reduce_fusion.1), kind=kOutput, calls=%fused_computation.34 | convolution fusion | flops 7453278208 | bytes 18391040 | tf_op jit(solution)/shard_map/ic,cyz->iyz/dot_general | solution.py:44
  250.5 24.9 %fusion.9 = f32[256,128,128]{2,1,0:T(8,128)} fusion(bf16[256,128,128]{2,0,1:T(8,128)(2,1)S(1)} %fusion.14, f32[128,168]{0,1:T(8,128)S(1)} %select_reduce_fusion.2), kind=kOutput, calls=%fused_computation.25 | convolution fusion | flops 3221225472 | bytes 25231360 | tf_op jit(solution)/shard_map/jc,xcz->xjz/dot_general | solution.py:44
  294.4 22.8 %bitcast_subtract_fusion = f32[256,128,128]{1,2,0:T(8,128)} fusion(f32[256,128,128]{1,2,0:T(8,128)} %copy.161, f32[256,128,128]{2,1,0:T(8,128)} %fusion.9, bf16[256,40,128]{2,0,1:T(8,128)(2,1)S(1)} %pad_maximum_fusion.8, f32[128,20]{0,1:T(8,128)S(1)} %copy-done.33, f32[128,20]{0,1:T(8,128)S(1)} %copy-done.32), kind=kOutput, calls=%fused_computation.6 | convolution fusion | flops 1019220992 | bytes 52973568 | tf_op jit(solution)/shard_map/jc,xcz->xjz/dot_general | solution.py:44
  356.3 66.1 %collective-permute-done.9 = bf16[16,256,128]{2,0,1:T(8,128)(2,1)} collective-permute-done((bf16[16,256,128]{2,0,1:T(8,128)(2,1)}, bf16[16,256,128]{2,0,1:T(8,128)(2,1)}, u32[]{:S(2)}, u32[]{:S(2)}) %collective-permute-start.9) | collective-permute-done | bytes 1048608 | tf_op jit(solution)/shard_map/ppermute | solution.py:64
  439.0 42.4 %collective-permute-start.11 = (bf16[16,128,128]{1,2,0:T(8,128)(2,1)S(1)}, bf16[16,128,128]{1,2,0:T(8,128)(2,1)S(1)}, u32[]{:S(2)}, u32[]{:S(2)}) collective-permute-start(bf16[16,128,128]{1,2,0:T(8,128)(2,1)S(1)} %get-tuple-element.69), channel_id=1, source_target_pairs={{0,1},{1,2},{2,3},{3,4},{4,5},{5,6},{6,7},{7,0},{8,9},{9,10},{10,1... | collective-permute-start | bytes 1572872 | tf_op jit(solution)/shard_map/ppermute | solution.py:64
  481.4 30.7 %collective-permute-done.29 = bf16[16,256,128]{2,0,1:T(8,128)(2,1)S(1)} collective-permute-done((bf16[16,256,128]{2,0,1:T(8,128)(2,1)S(1)}, bf16[16,256,128]{2,0,1:T(8,128)(2,1)S(1)}, u32[]{:S(2)}, u32[]{:S(2)}) %collective-permute-start.29) | collective-permute-done | bytes 1048608 | tf_op jit(solution)/shard_map/ppermute | solution.py:64
  532.6 22.0 %collective-permute-done.13 = bf16[16,128,128]{1,2,0:T(8,128)(2,1)S(1)} collective-permute-done((bf16[16,128,128]{1,2,0:T(8,128)(2,1)S(1)}, bf16[16,128,128]{1,2,0:T(8,128)(2,1)S(1)}, u32[]{:S(2)}, u32[]{:S(2)}) %collective-permute-start.13) | collective-permute-done | bytes 524320 | tf_op jit(solution)/shard_map/ppermute | solution.py:64
  554.8 17.2 %collective-permute-start.33 = (bf16[16,128,128]{1,2,0:T(8,128)(2,1)}, bf16[16,128,128]{1,2,0:T(8,128)(2,1)}, u32[]{:S(2)}, u32[]{:S(2)}) collective-permute-start(bf16[16,128,128]{1,2,0:T(8,128)(2,1)} %get-tuple-element.43), channel_id=1, source_target_pairs={{0,3},{1,4},{2,5},{3,6},{4,7},{5,0},{6,1},{7,2},{8,11},{9,12},{10,... | collective-permute-start | bytes 1572872 | tf_op jit(solution)/shard_map/ppermute | solution.py:64
  717.1 59.2 %collective-permute-done.25 = bf16[16,256,128]{1,2,0:T(8,128)(2,1)S(1)} collective-permute-done((bf16[16,256,128]{1,2,0:T(8,128)(2,1)S(1)}, bf16[16,256,128]{1,2,0:T(8,128)(2,1)S(1)}, u32[]{:S(2)}, u32[]{:S(2)}) %collective-permute-start.25) | collective-permute-done | bytes 1048608 | tf_op jit(solution)/shard_map/ppermute | solution.py:64
  777.4 20.1 %collective-permute-done.26 = bf16[16,256,128]{1,2,0:T(8,128)(2,1)S(1)} collective-permute-done((bf16[16,256,128]{1,2,0:T(8,128)(2,1)S(1)}, bf16[16,256,128]{1,2,0:T(8,128)(2,1)S(1)}, u32[]{:S(2)}, u32[]{:S(2)}) %collective-permute-start.26) | collective-permute-done | bytes 1048608 | tf_op jit(solution)/shard_map/ppermute | solution.py:64
  805.3 23.9 %collective-permute-done.45 = bf16[16,256,128]{1,2,0:T(8,128)(2,1)S(1)} collective-permute-done((bf16[16,256,128]{1,2,0:T(8,128)(2,1)S(1)}, bf16[16,256,128]{1,2,0:T(8,128)(2,1)S(1)}, u32[]{:S(2)}, u32[]{:S(2)}) %collective-permute-start.45) | collective-permute-done | bytes 1048608 | tf_op jit(solution)/shard_map/ppermute | solution.py:64
  830.3 40.5 %collective-permute-done.46 = bf16[16,256,128]{1,2,0:T(8,128)(2,1)S(1)} collective-permute-done((bf16[16,256,128]{1,2,0:T(8,128)(2,1)S(1)}, bf16[16,256,128]{1,2,0:T(8,128)(2,1)S(1)}, u32[]{:S(2)}, u32[]{:S(2)}) %collective-permute-start.46) | collective-permute-done | bytes 1048608 | tf_op jit(solution)/shard_map/ppermute | solution.py:64
  893.6 23.9 %collective-permute-start.48 = (bf16[20,128,128]{2,1,0:T(8,128)(2,1)S(1)}, bf16[20,128,128]{2,1,0:T(8,128)(2,1)S(1)}, u32[]{:S(2)}, u32[]{:S(2)}) collective-permute-start(bf16[20,128,128]{2,1,0:T(8,128)(2,1)S(1)} %get-tuple-element.17), channel_id=1, source_target_pairs={{0,8},{8,16},{16,24},{1,9},{9,17},{17,25},{2,10},{10,18},{18,26},{... | collective-permute-start | bytes 1966088 | tf_op jit(solution)/shard_map/ppermute | solution.py:19
  927.8 17.4 %copy.155 = f32[256,128,128]{1,2,0:T(8,128)} copy(f32[256,128,128]{2,1,0:T(8,128)} %get-tuple-element.128) | data formatting | bytes 33554432 | tf_op jit(solution)/shard_map/kxy,zk->xyz/dot_general | solution.py:162
  956.6 23.8 %fusion.17 = bf16[256,128,128]{2,0,1:T(8,128)(2,1)} fusion(bf16[296,128,128]{2,1,0:T(8,128)(2,1)} %pad_maximum_fusion.2, f32[256,296]{0,1:T(8,128)S(1)} %copy-done.12), kind=kOutput, calls=%fused_computation.35 | convolution fusion | flops 7453278208 | bytes 18391040 | tf_op jit(solution)/shard_map/ic,cyz->iyz/dot_general | solution.py:44
  994.5 16.8 %fusion.7 = f32[256,128,128]{2,1,0:T(8,128)} fusion(bf16[256,128,128]{2,0,1:T(8,128)(2,1)} %fusion.17, f32[128,168]{0,1:T(8,128)S(1)} %copy-done.14), kind=kOutput, calls=%fused_computation.23 | convolution fusion | flops 3221225472 | bytes 25231360 | tf_op jit(solution)/shard_map/jc,xcz->xjz/dot_general | solution.py:44
  1012.0 21.0 %fusion.1 = (f32[]{:T(128)}, f32[256,128,128]{2,1,0:T(8,128)}) fusion(bf16[256,128,128]{1,2,0:T(8,128)(2,1)} %copy.125, f32[256,128,128]{2,1,0:T(8,128)} %fusion.7, f32[128,20]{0,1:T(8,128)S(1)} %copy-done.25, f32[128,20]{0,1:T(8,128)S(1)} %copy-done.23, bf16[256,40,128]{2,0,1:T(8,128)(2,1)S(1)} %pad_maximum_fusion.9), kind=kOutput, calls=%fused_computation.3 | convolution fusion | flops 1027609600 | bytes 44584964 | tf_op jit(solution)/shard_map/jc,xcz->xjz/dot_general | solution.py:44
  1033.1 45.3 %all-reduce = (f32[]{:T(128)}, f32[]{:T(128)}, f32[]{:T(128)}) all-reduce(f32[]{:T(128)} %multiply_reduce_fusion.1, f32[]{:T(128)} %get-tuple-element.125, f32[]{:T(128)} %get-tuple-element.127), channel_id=1, replica_groups=mesh['gx'=4,'gy'=8] {'gx','gy'}, use_global_device_ids=true, to_apply=%region_9.10 | all-reduce | flops 3 | bytes 24 | tf_op jit(solution)/shard_map/psum | solution.py:169
  1080.3 17.3 %multiply_add_fusion = f32[256,128,128]{1,2,0:T(8,128)} fusion(f32[256,128,128]{1,2,0:T(8,128)} %copy.161, f32[256,128,128]{1,2,0:T(8,128)} %copy.155, f32[]{:T(128)S(6)} %div.21), kind=kLoop, calls=%fused_computation.8 | loop fusion | flops 8388608 | bytes 50331652 | tf_op jit(solution)/shard_map/add | solution.py:176
  1114.1 17.4 %copy.162 = f32[256,128,128]{2,1,0:T(8,128)} copy(f32[256,128,128]{1,2,0:T(8,128)} %multiply_add_fusion) | data formatting | bytes 33554432
  1131.5 17.4 %copy.163 = f32[256,128,128]{2,1,0:T(8,128)} copy(f32[256,128,128]{1,2,0:T(8,128)} %fusion.2) | data formatting | bytes 33554432
  (344 shorter events, 479.0 us)
Async XLA Ops:
  7.2 268.2 %all-gather.4.cloned.1.call-start = ((), (), s32[]{:S(2)}) async-start(), calls=%async_computation | async-start | bytes 2621440 | tf_op jit(solution)/shard_map/all_gather | solution.py:109
  7.9 279.4 %all-gather.6.cloned.1.call-start = ((), (), s32[]{:S(2)}) async-start(), calls=%async_computation.1 | async-start | bytes 2359296 | tf_op jit(solution)/shard_map/all_gather | solution.py:110
  331.7 90.7 %collective-permute-start.9 = (bf16[16,256,128]{2,0,1:T(8,128)(2,1)}, bf16[16,256,128]{2,0,1:T(8,128)(2,1)}, u32[]{:S(2)}, u32[]{:S(2)}) collective-permute-start(bf16[16,256,128]{2,0,1:T(8,128)(2,1)} %get-tuple-element.73), channel_id=1, source_target_pairs={{0,16},{8,24},{16,0},{24,8},{1,17},{9,25},{17,1},{25,9},{2,18},{10... | collective-permute-start | bytes 3145736 | tf_op jit(solution)/shard_map/ppermute | solution.py:64
  332.3 90.1 %collective-permute-start.8 = (bf16[16,256,128]{2,0,1:T(8,128)(2,1)S(1)}, bf16[16,256,128]{2,0,1:T(8,128)(2,1)}, u32[]{:S(2)}, u32[]{:S(2)}) collective-permute-start(bf16[16,256,128]{2,0,1:T(8,128)(2,1)S(1)} %get-tuple-element.74), channel_id=1, source_target_pairs={{0,8},{8,16},{16,24},{24,0},{1,9},{9,17},{17,25},{25,1},{2,10},{10... | collective-permute-start | bytes 3145736 | tf_op jit(solution)/shard_map/ppermute | solution.py:64
  339.9 141.5 %collective-permute-start.30 = (bf16[16,256,128]{2,0,1:T(8,128)(2,1)S(1)}, bf16[16,256,128]{2,0,1:T(8,128)(2,1)S(1)}, u32[]{:S(2)}, u32[]{:S(2)}) collective-permute-start(bf16[16,256,128]{2,0,1:T(8,128)(2,1)S(1)} %get-tuple-element.48), channel_id=1, source_target_pairs={{0,24},{8,0},{16,8},{24,16},{1,25},{9,1},{17,9},{25,17},{2,26},{10... | collective-permute-start | bytes 3145736 | tf_op jit(solution)/shard_map/ppermute | solution.py:64
  342.4 169.6 %collective-permute-start.29 = (bf16[16,256,128]{2,0,1:T(8,128)(2,1)S(1)}, bf16[16,256,128]{2,0,1:T(8,128)(2,1)S(1)}, u32[]{:S(2)}, u32[]{:S(2)}) collective-permute-start(bf16[16,256,128]{2,0,1:T(8,128)(2,1)S(1)} %get-tuple-element.49), channel_id=1, source_target_pairs={{0,16},{8,24},{16,0},{24,8},{1,17},{9,25},{17,1},{25,9},{2,18},{10... | collective-permute-start | bytes 3145736 | tf_op jit(solution)/shard_map/ppermute | solution.py:64
  356.3 155.8 %collective-permute-start.28 = (bf16[16,256,128]{2,0,1:T(8,128)(2,1)S(1)}, bf16[16,256,128]{2,0,1:T(8,128)(2,1)S(1)}, u32[]{:S(2)}, u32[]{:S(2)}) collective-permute-start(bf16[16,256,128]{2,0,1:T(8,128)(2,1)S(1)} %get-tuple-element.50), channel_id=1, source_target_pairs={{0,8},{8,16},{16,24},{24,0},{1,9},{9,17},{17,25},{25,1},{2,10},{10... | collective-permute-start | bytes 3145736 | tf_op jit(solution)/shard_map/ppermute | solution.py:64
  433.0 99.4 %collective-permute-start.12 = (bf16[16,128,128]{1,2,0:T(8,128)(2,1)S(1)}, bf16[16,128,128]{1,2,0:T(8,128)(2,1)S(1)}, u32[]{:S(2)}, u32[]{:S(2)}) collective-permute-start(bf16[16,128,128]{1,2,0:T(8,128)(2,1)S(1)} %get-tuple-element.68), channel_id=1, source_target_pairs={{0,2},{1,3},{2,4},{3,5},{4,6},{5,7},{6,0},{7,1},{8,10},{9,11},{10,... | collective-permute-start | bytes 1572872 | tf_op jit(solution)/shard_map/ppermute | solution.py:64
  439.0 90.0 %collective-permute-start.11 = (bf16[16,128,128]{1,2,0:T(8,128)(2,1)S(1)}, bf16[16,128,128]{1,2,0:T(8,128)(2,1)S(1)}, u32[]{:S(2)}, u32[]{:S(2)}) collective-permute-start(bf16[16,128,128]{1,2,0:T(8,128)(2,1)S(1)} %get-tuple-element.69), channel_id=1, source_target_pairs={{0,1},{1,2},{2,3},{3,4},{4,5},{5,6},{6,7},{7,0},{8,9},{9,10},{10,1... | collective-permute-start | bytes 1572872 | tf_op jit(solution)/shard_map/ppermute | solution.py:64
  532.4 44.8 %collective-permute-start.17 = (bf16[16,128,128]{1,2,0:T(8,128)(2,1)S(1)}, bf16[16,128,128]{1,2,0:T(8,128)(2,1)S(1)}, u32[]{:S(2)}, u32[]{:S(2)}) collective-permute-start(bf16[16,128,128]{1,2,0:T(8,128)(2,1)S(1)} %get-tuple-element.63), channel_id=1, source_target_pairs={{0,7},{1,0},{2,1},{3,2},{4,3},{5,4},{6,5},{7,6},{8,15},{9,8},{10,9... | collective-permute-start | bytes 1572872 | tf_op jit(solution)/shard_map/ppermute | solution.py:64
  554.6 58.9 %collective-permute-start.35 = (bf16[16,128,128]{1,2,0:T(8,128)(2,1)}, bf16[16,128,128]{1,2,0:T(8,128)(2,1)}, u32[]{:S(2)}, u32[]{:S(2)}) collective-permute-start(bf16[16,128,128]{1,2,0:T(8,128)(2,1)} %get-tuple-element.41), channel_id=1, source_target_pairs={{0,5},{1,6},{2,7},{3,0},{4,1},{5,2},{6,3},{7,4},{8,13},{9,14},{10,... | collective-permute-start | bytes 1572872 | tf_op jit(solution)/shard_map/ppermute | solution.py:64
  554.7 57.1 %collective-permute-start.34 = (bf16[16,128,128]{1,2,0:T(8,128)(2,1)}, bf16[16,128,128]{1,2,0:T(8,128)(2,1)}, u32[]{:S(2)}, u32[]{:S(2)}) collective-permute-start(bf16[16,128,128]{1,2,0:T(8,128)(2,1)} %get-tuple-element.42), channel_id=1, source_target_pairs={{0,4},{1,5},{2,6},{3,7},{4,0},{5,1},{6,2},{7,3},{8,12},{9,13},{10,... | collective-permute-start | bytes 1572872 | tf_op jit(solution)/shard_map/ppermute | solution.py:64
  554.8 55.8 %collective-permute-start.33 = (bf16[16,128,128]{1,2,0:T(8,128)(2,1)}, bf16[16,128,128]{1,2,0:T(8,128)(2,1)}, u32[]{:S(2)}, u32[]{:S(2)}) collective-permute-start(bf16[16,128,128]{1,2,0:T(8,128)(2,1)} %get-tuple-element.43), channel_id=1, source_target_pairs={{0,3},{1,4},{2,5},{3,6},{4,7},{5,0},{6,1},{7,2},{8,11},{9,12},{10,... | collective-permute-start | bytes 1572872 | tf_op jit(solution)/shard_map/ppermute | solution.py:64
  610.7 51.0 %collective-permute-start.22 = (bf16[16,128,128]{2,1,0:T(8,128)(2,1)}, bf16[16,128,128]{2,1,0:T(8,128)(2,1)}, u32[]{:S(2)}, u32[]{:S(2)}) collective-permute-start(bf16[16,128,128]{2,1,0:T(8,128)(2,1)} %get-tuple-element.57), channel_id=1, source_target_pairs={{0,5},{1,6},{2,7},{3,0},{4,1},{5,2},{6,3},{7,4},{8,13},{9,14},{10,... | collective-permute-start | bytes 1572872 | tf_op jit(solution)/shard_map/ppermute | solution.py:64
  611.8 47.1 %collective-permute-start.21 = (bf16[16,128,128]{2,1,0:T(8,128)(2,1)}, bf16[16,128,128]{2,1,0:T(8,128)(2,1)}, u32[]{:S(2)}, u32[]{:S(2)}) collective-permute-start(bf16[16,128,128]{2,1,0:T(8,128)(2,1)} %get-tuple-element.58), channel_id=1, source_target_pairs={{0,4},{1,5},{2,6},{3,7},{4,0},{5,1},{6,2},{7,3},{8,12},{9,13},{10,... | collective-permute-start | bytes 1572872 | tf_op jit(solution)/shard_map/ppermute | solution.py:64
  613.5 44.2 %collective-permute-start.20 = (bf16[16,128,128]{2,1,0:T(8,128)(2,1)}, bf16[16,128,128]{2,1,0:T(8,128)(2,1)}, u32[]{:S(2)}, u32[]{:S(2)}) collective-permute-start(bf16[16,128,128]{2,1,0:T(8,128)(2,1)} %get-tuple-element.59), channel_id=1, source_target_pairs={{0,3},{1,4},{2,5},{3,6},{4,7},{5,0},{6,1},{7,2},{8,11},{9,12},{10,... | collective-permute-start | bytes 1572872 | tf_op jit(solution)/shard_map/ppermute | solution.py:64
  657.7 51.1 %collective-permute-start.42 = (bf16[16,128,128]{2,1,0:T(8,128)(2,1)S(1)}, bf16[16,128,128]{2,1,0:T(8,128)(2,1)S(1)}, u32[]{:S(2)}, u32[]{:S(2)}) collective-permute-start(bf16[16,128,128]{2,1,0:T(8,128)(2,1)S(1)} %get-tuple-element.33), channel_id=1, source_target_pairs={{0,5},{1,6},{2,7},{3,0},{4,1},{5,2},{6,3},{7,4},{8,13},{9,14},{10,... | collective-permute-start | bytes 1572872 | tf_op jit(solution)/shard_map/ppermute | solution.py:64
  658.9 46.8 %collective-permute-start.41 = (bf16[16,128,128]{2,1,0:T(8,128)(2,1)S(1)}, bf16[16,128,128]{2,1,0:T(8,128)(2,1)S(1)}, u32[]{:S(2)}, u32[]{:S(2)}) collective-permute-start(bf16[16,128,128]{2,1,0:T(8,128)(2,1)S(1)} %get-tuple-element.34), channel_id=1, source_target_pairs={{0,4},{1,5},{2,6},{3,7},{4,0},{5,1},{6,2},{7,3},{8,12},{9,13},{10,... | collective-permute-start | bytes 1572872 | tf_op jit(solution)/shard_map/ppermute | solution.py:64
  705.6 93.1 %collective-permute-start.27 = (bf16[16,256,128]{1,2,0:T(8,128)(2,1)S(1)}, bf16[16,256,128]{1,2,0:T(8,128)(2,1)S(1)}, u32[]{:S(2)}, u32[]{:S(2)}) collective-permute-start(bf16[16,256,128]{1,2,0:T(8,128)(2,1)S(1)} %get-tuple-element.51), channel_id=1, source_target_pairs={{0,24},{8,0},{16,8},{24,16},{1,25},{9,1},{17,9},{25,17},{2,26},{10... | collective-permute-start | bytes 3145736 | tf_op jit(solution)/shard_map/ppermute | solution.py:64
  705.7 91.9 %collective-permute-start.26 = (bf16[16,256,128]{1,2,0:T(8,128)(2,1)S(1)}, bf16[16,256,128]{1,2,0:T(8,128)(2,1)S(1)}, u32[]{:S(2)}, u32[]{:S(2)}) collective-permute-start(bf16[16,256,128]{1,2,0:T(8,128)(2,1)S(1)} %get-tuple-element.52), channel_id=1, source_target_pairs={{0,16},{8,24},{16,0},{24,8},{1,17},{9,25},{17,1},{25,9},{2,18},{10... | collective-permute-start | bytes 3145736 | tf_op jit(solution)/shard_map/ppermute | solution.py:64
  708.8 67.5 %collective-permute-start.25 = (bf16[16,256,128]{1,2,0:T(8,128)(2,1)S(1)}, bf16[16,256,128]{1,2,0:T(8,128)(2,1)S(1)}, u32[]{:S(2)}, u32[]{:S(2)}) collective-permute-start(bf16[16,256,128]{1,2,0:T(8,128)(2,1)S(1)} %get-tuple-element.53), channel_id=1, source_target_pairs={{0,8},{8,16},{16,24},{24,0},{1,9},{9,17},{17,25},{25,1},{2,10},{10... | collective-permute-start | bytes 3145736 | tf_op jit(solution)/shard_map/ppermute | solution.py:64
  801.2 69.5 %collective-permute-start.46 = (bf16[16,256,128]{1,2,0:T(8,128)(2,1)S(1)}, bf16[16,256,128]{1,2,0:T(8,128)(2,1)S(1)}, u32[]{:S(2)}, u32[]{:S(2)}) collective-permute-start(bf16[16,256,128]{1,2,0:T(8,128)(2,1)S(1)} %get-tuple-element.28), channel_id=1, source_target_pairs={{0,16},{8,24},{16,0},{24,8},{1,17},{9,25},{17,1},{25,9},{2,18},{10... | collective-permute-start | bytes 3145736 | tf_op jit(solution)/shard_map/ppermute | solution.py:64
  802.1 69.7 %collective-permute-start.47 = (bf16[16,256,128]{1,2,0:T(8,128)(2,1)S(1)}, bf16[16,256,128]{1,2,0:T(8,128)(2,1)S(1)}, u32[]{:S(2)}, u32[]{:S(2)}) collective-permute-start(bf16[16,256,128]{1,2,0:T(8,128)(2,1)S(1)} %get-tuple-element.27), channel_id=1, source_target_pairs={{0,24},{8,0},{16,8},{24,16},{1,25},{9,1},{17,9},{25,17},{2,26},{10... | collective-permute-start | bytes 3145736 | tf_op jit(solution)/shard_map/ppermute | solution.py:64
  893.6 51.6 %collective-permute-start.48 = (bf16[20,128,128]{2,1,0:T(8,128)(2,1)S(1)}, bf16[20,128,128]{2,1,0:T(8,128)(2,1)S(1)}, u32[]{:S(2)}, u32[]{:S(2)}) collective-permute-start(bf16[20,128,128]{2,1,0:T(8,128)(2,1)S(1)} %get-tuple-element.17), channel_id=1, source_target_pairs={{0,8},{8,16},{16,24},{1,9},{9,17},{17,25},{2,10},{10,18},{18,26},{... | collective-permute-start | bytes 1966088 | tf_op jit(solution)/shard_map/ppermute | solution.py:19
  (80 other events, 1937.7 us)
Sparse Core Ops, SparseCore 0:
  9.6 59.0 all-gather.3
  70.6 30.1 all-gather.5

commit v2 on v1

--- a/solution.py
+++ b/solution.py
@@ -5,7 +5,7 @@
 
 HALF = 16
 SHIFT = 4
-CHUNKS = 2
+CHUNKS = 4
 
 
 highest = lax.Precision.HIGHEST
@@ -74,10 +74,11 @@
     extended = jnp.concatenate([low, along_z, high], axis=0)
     along_x = split_dot("ic,cyz->iyz", x_matrix, extended).astype(jnp.bfloat16)
     low, high = exchange(along_x, "gy", 1, rim)
-    inner = split_dot("jc,xcz->xjz", y_matrix[:, rim:-rim], along_x)
+    spread = jnp.broadcast_to(y_matrix, (block_x,) + y_matrix.shape)
+    inner = split_dot("xjc,xcz->xjz", spread[:, :, rim:-rim], along_x)
     rims = jnp.concatenate([low, high], axis=1)
-    rim_matrix = jnp.concatenate([y_matrix[:, :rim], y_matrix[:, -rim:]], axis=1)
-    return inner + split_dot("jc,xcz->xjz", rim_matrix, rims)
+    rim_matrix = jnp.concatenate([spread[:, :, :rim], spread[:, :, -rim:]], axis=2)
+    return inner + split_dot("xjc,xcz->xjz", rim_matrix, rims)
 
 
 def apply_blur(source, kernels, offsets):
@@ -165,13 +166,14 @@
     along_z = jnp.einsum(
         "kxy,zk->xyz", section_six.astype(jnp.float32), z_modes, precision=lax.Precision.HIGH
     ).astype(jnp.bfloat16)
-    local_descent = jnp.sum(gradient * direction)
-    descent = lax.psum(local_descent, ("gx", "gy"))
     blurred = blur_xy(along_z, kernels, offsets)
-    data_sum, norm_sum = lax.psum(
-        (jnp.sum(weights * blurred * blurred), jnp.sum(direction * direction)), ("gx", "gy")
-    )
-    energy = data_sum + tikhonov * norm_sum
+    local = jnp.stack(
+        [
+            jnp.sum(gradient * direction),
+            jnp.sum(weights * blurred * blurred) + tikhonov * jnp.sum(direction * direction),
+        ]
+    )
+    descent, energy = jnp.sum(lax.all_gather(local, ("gx", "gy")), axis=0)
     step_size = descent / energy
     return (iterate + step_size * direction, misfit - step_size * blurred)
 

time: 1160 us -> 1200 us (1.034)
  starting transfers between devices: 157 us -> 262 us
  local copies, waits for them, and re-layouts: 201 us -> 137 us
  waiting for transfers between devices: 341 us -> 288 us
  blocking collectives: 56 us -> 84.4 us
  matrix products: 298 us -> 319 us
    ppermute x40 -> x80, starting transfers between devices: 109 us -> 223 us  [swap(): arrived.append(lax.ppermute(pieces[step], axis_name, pairs))]
    ppermute x40 -> x80, waiting for transfers between devices: 335 us -> 274 us  [swap(): arrived.append(lax.ppermute(pieces[step], axis_name, pairs))]
    unnamed x163 -> x217, local copies, waits for them, and re-layouts: 118 us -> 67.2 us
    unnamed x0 -> x1, blocking collectives: none -> 46.4 us
    psum x1 -> x0, blocking collectives: 45.3 us -> none  [shards(): descent = lax.psum(local_descent, ('gx', 'gy'))]
    all_gather x1, blocking collectives: 10.7 us -> 38 us  [shards(): all_x = lax.all_gather(eigen_x, 'gx', axis=0, tiled=True)]
    dot_general x1 -> x0, local copies, waits for them, and re-layouts: 17.4 us -> none  [shards(): jnp.einsum('kxy,zk->xyz', section_six, basis_z, preferred_element_type=jn...]
    dot_general x9, matrix products: 187 us -> 200 us  [split_dot(): jnp.einsum(spec, matrix, block.astype(jnp.float32), precision=lax.Precisi...]
  transfers between devices with their start and end apart: 54 -> 94, of which waited for: 20 -> 32; matrix products, arithmetic and copies ran while one was open for 33% -> 30% of each run, Pallas kernels for 0% -> 0%
where the time goes in v2:
time: 1200 us; the launch traced here: 1190 us
  matrix products  319 us (27%)
  waiting for transfers between devices  288 us (24%)
  starting transfers between devices  262 us (22%)
  local copies, waits for them, and re-layouts  137 us (11%)
  blocking collectives  84.4 us (7%)
  other arithmetic  77.2 us (6%)
  between operations  18.9 us (2%)
    ppermute x80, waiting for transfers between devices, swap(): arrived.append(lax.ppermute(pieces[step], axis_name, pairs))  274 us
    ppermute x80, starting transfers between devices, swap(): arrived.append(lax.ppermute(pieces[step], axis_name, pairs))  223 us
    dot_general x9, matrix products, split_dot(): jnp.einsum(spec, matrix, block.astype(jnp.float32), precision=lax.Precisi...  200 us
    unnamed x217, local copies, waits for them, and re-layouts  67.2 us
    unnamed x1, blocking collectives  46.4 us
    all_gather x1, blocking collectives, shards(): all_x = lax.all_gather(eigen_x, 'gx', axis=0, tiled=True)  38 us
    dot_general x4, matrix products, shards(): jnp.einsum('axk,jk->axj', section_four, y_ahead, preferred_element_type=j...  33.2 us
    ppermute x6, starting transfers between devices, exchange(): lax.ppermute(lax.slice_in_dim(block, block.shape[dim] - width, None, axis...  30 us
  transfers between devices with their start and end apart: 94, of which 32 were waited for; matrix products, arithmetic and copies ran while one was open for 30% of the time, Pallas kernels for 0%

profile of v2, /device:TPU:0, one launch (start us, length us, event | category | flops | bytes accessed | tf_op | source)
XLA Modules:
  0.0 1186.5 jit_solution(15547967778899269092)
XLA Ops:
  36.5 38.0 %all-gather.1 = f32[4,1,256]{2,1,0:T(1,128)S(1)} all-gather(f32[1,1,256]{2,1,0:T(1,128)S(1)} %bitcast.177), channel_id=1, replica_groups=mesh['gx'=4,'gy'=8] {'gx'}, dimensions={0}, use_global_device_ids=true | all-gather | bytes 5120 | tf_op jit(solution)/shard_map/all_gather | solution.py:121
  95.6 14.1 %copy.106 = bf16[296,128,128]{2,0,1:T(8,128)(2,1)} copy(bf16[296,128,128]{1,2,0:T(8,128)(2,1)} %pad_maximum_fusion) | data formatting | bytes 19398656 | tf_op jit(solution)/shard_map/concatenate | solution.py:74
  124.8 24.1 %fusion.10 = f32[256,128,128]{2,1,0:T(8,128)} fusion(bf16[256,128,128]{2,0,1:T(8,128)(2,1)S(1)} %convolution_convert_fusion.1, f32[128,128]{1,0:T(8,128)S(1)} %copy.105), kind=kOutput, calls=%fused_computation.26 | convolution fusion | flops 3221225472 | bytes 25231360 | tf_op jit(solution)/shard_map/xjc,xcz->xjz/dot_general | solution.py:44
  152.8 18.2 %add_subtract_fusion = f32[256,128,128]{2,1,0:T(8,128)} fusion(f32[256,128,128]{2,1,0:T(8,128)} %fusion.10, bf16[256,128,128]{2,1,0:T(8,128)(2,1)} %param.12, f32[256,128,20]{1,2,0:T(8,128)} %broadcast_in_dim.157, f32[256,128,20]{1,2,0:T(8,128)S(1)} %broadcast_in_dim.156, bf16[256,40,128]{2,0,1:T(8,128)(2,1)} %pad_maximum_fusion.8), kind=kOutput, calls=%fused_computation.9 | convolution fusion | flops 1020526592 | bytes 49807360 | tf_op jit(solution)/shard_map/xjc,xcz->xjz/dot_general | solution.py:44
  171.0 13.8 %fusion.15 = bf16[256,128,128]{2,1,0:T(8,128)(2,1)} fusion(f32[256,128,128]{2,1,0:T(8,128)} %add_subtract_fusion, bf16[256,128,128]{2,1,0:T(8,128)(2,1)} %param.13, f32[128,128]{1,0:T(8,128)} %select_reduce_fusion.4), kind=kOutput, calls=%fused_computation.33 | convolution fusion | flops 3233808384 | bytes 33619968 | tf_op jit(solution)/shard_map/xyc,zc->xyz/dot_general | solution.py:87
  208.8 26.6 %fusion.16 = bf16[256,128,128]{2,0,1:T(8,128)(2,1)S(1)} fusion(bf16[296,128,128]{2,1,0:T(8,128)(2,1)S(1)} %pad_maximum_fusion.1, f32[256,296]{0,1:T(8,128)S(1)} %select_reduce_fusion.1), kind=kOutput, calls=%fused_computation.34 | convolution fusion | flops 7453278208 | bytes 18391040 | tf_op jit(solution)/shard_map/ic,cyz->iyz/dot_general | solution.py:44
  245.1 24.5 %fusion.8 = f32[256,128,128]{2,1,0:T(8,128)} fusion(bf16[256,128,128]{2,0,1:T(8,128)(2,1)S(1)} %fusion.16, f32[128,128]{1,0:T(8,128)S(1)} %copy.104), kind=kOutput, calls=%fused_computation.24 | convolution fusion | flops 3221225472 | bytes 25231360 | tf_op jit(solution)/shard_map/xjc,xcz->xjz/dot_general | solution.py:44
  291.2 25.5 %fusion.163 = (bf16[256,128,128]{2,1,0:T(8,128)(2,1)}, f32[256,128,128]{2,1,0:T(8,128)}) fusion(f32[256,128,128]{2,1,0:T(8,128)} %param.14, f32[256,128,128]{2,1,0:T(8,128)} %fusion.8, bf16[256,40,128]{2,0,1:T(8,128)(2,1)} %pad_maximum_fusion.9, f32[256,128,20]{1,2,0:T(8,128)S(1)} %broadcast_in_dim.161, f32[256,128,20]{1,2,0:T(8,128)S(1)} %broadcast_in_dim.160), kind=kOutput, calls=%fused_computation.317 | convolution fusion | flops 1024720896 | bytes 66584576 | tf_op jit(solution)/shard_map/xjc,xcz->xjz/dot_general | solution.py:44
  344.6 33.1 %collective-permute-done.69 = bf16[8,256,128]{2,0,1:T(8,128)(2,1)S(1)} collective-permute-done((bf16[8,256,128]{2,0,1:T(8,128)(2,1)S(1)}, bf16[8,256,128]{2,0,1:T(8,128)(2,1)S(1)}, u32[]{:S(2)}, u32[]{:S(2)}) %collective-permute-start.69) | collective-permute-done | bytes 524320 | tf_op jit(solution)/shard_map/ppermute | solution.py:64
  377.9 32.3 %collective-permute-start.29 = (bf16[8,256,128]{2,0,1:T(8,128)(2,1)S(1)}, bf16[8,256,128]{2,0,1:T(8,128)(2,1)S(1)}, u32[]{:S(2)}, u32[]{:S(2)}) collective-permute-start(bf16[8,256,128]{2,0,1:T(8,128)(2,1)S(1)} %get-tuple-element.88), channel_id=1, source_target_pairs={{0,16},{8,24},{16,0},{24,8},{1,17},{9,25},{17,1},{25,9},{2,18},{10... | collective-permute-start | bytes 1572872 | tf_op jit(solution)/shard_map/ppermute | solution.py:64
  414.6 29.7 %collective-permute-done.49 = bf16[8,256,128]{2,0,1:T(8,128)(2,1)S(1)} collective-permute-done((bf16[8,256,128]{2,0,1:T(8,128)(2,1)S(1)}, bf16[8,256,128]{2,0,1:T(8,128)(2,1)S(1)}, u32[]{:S(2)}, u32[]{:S(2)}) %collective-permute-start.49) | collective-permute-done | bytes 524320 | tf_op jit(solution)/shard_map/ppermute | solution.py:64
  461.7 27.5 %collective-permute-done.29 = bf16[8,256,128]{2,0,1:T(8,128)(2,1)S(1)} collective-permute-done((bf16[8,256,128]{2,0,1:T(8,128)(2,1)S(1)}, bf16[8,256,128]{2,0,1:T(8,128)(2,1)S(1)}, u32[]{:S(2)}, u32[]{:S(2)}) %collective-permute-start.29) | collective-permute-done | bytes 524320 | tf_op jit(solution)/shard_map/ppermute | solution.py:64
  773.4 17.6 %collective-permute-done.25 = bf16[8,256,128]{1,2,0:T(8,128)(2,1)S(1)} collective-permute-done((bf16[8,256,128]{1,2,0:T(8,128)(2,1)S(1)}, bf16[8,256,128]{1,2,0:T(8,128)(2,1)S(1)}, u32[]{:S(2)}, u32[]{:S(2)}) %collective-permute-start.25) | collective-permute-done | bytes 524320 | tf_op jit(solution)/shard_map/ppermute | solution.py:64
  834.3 21.8 %collective-permute-done.46 = bf16[8,256,128]{1,2,0:T(8,128)(2,1)S(1)} collective-permute-done((bf16[8,256,128]{1,2,0:T(8,128)(2,1)S(1)}, bf16[8,256,128]{1,2,0:T(8,128)(2,1)S(1)}, u32[]{:S(2)}, u32[]{:S(2)}) %collective-permute-start.46) | collective-permute-done | bytes 524320 | tf_op jit(solution)/shard_map/ppermute | solution.py:64
  858.8 14.6 %collective-permute-start.67 = (bf16[8,256,128]{1,2,0:T(8,128)(2,1)S(1)}, bf16[8,256,128]{1,2,0:T(8,128)(2,1)S(1)}, u32[]{:S(2)}, u32[]{:S(2)}) collective-permute-start(bf16[8,256,128]{1,2,0:T(8,128)(2,1)S(1)} %get-tuple-element.42), channel_id=1, source_target_pairs={{0,24},{8,0},{16,8},{24,16},{1,25},{9,1},{17,9},{25,17},{2,26},{10... | collective-permute-start | bytes 1572872 | tf_op jit(solution)/shard_map/ppermute | solution.py:64
  876.3 30.0 %collective-permute-done.65 = bf16[8,256,128]{1,2,0:T(8,128)(2,1)S(1)} collective-permute-done((bf16[8,256,128]{1,2,0:T(8,128)(2,1)S(1)}, bf16[8,256,128]{1,2,0:T(8,128)(2,1)S(1)}, u32[]{:S(2)}, u32[]{:S(2)}) %collective-permute-start.65) | collective-permute-done | bytes 524320 | tf_op jit(solution)/shard_map/ppermute | solution.py:64
  937.1 18.8 %collective-permute-done.86 = bf16[8,256,128]{1,2,0:T(8,128)(2,1)S(1)} collective-permute-done((bf16[8,256,128]{1,2,0:T(8,128)(2,1)S(1)}, bf16[8,256,128]{1,2,0:T(8,128)(2,1)S(1)}, u32[]{:S(2)}, u32[]{:S(2)}) %collective-permute-start.86) | collective-permute-done | bytes 524320 | tf_op jit(solution)/shard_map/ppermute | solution.py:64
  981.8 13.6 %collective-permute-start.88 = (bf16[20,128,128]{2,1,0:T(8,128)(2,1)S(1)}, bf16[20,128,128]{2,1,0:T(8,128)(2,1)S(1)}, u32[]{:S(2)}, u32[]{:S(2)}) collective-permute-start(bf16[20,128,128]{2,1,0:T(8,128)(2,1)S(1)} %get-tuple-element.8), channel_id=1, source_target_pairs={{0,8},{8,16},{16,24},{1,9},{9,17},{17,25},{2,10},{10,18},{18,26},{... | collective-permute-start | bytes 1966088 | tf_op jit(solution)/shard_map/ppermute | solution.py:19
  1019.6 26.6 %fusion.19 = bf16[256,128,128]{2,0,1:T(8,128)(2,1)S(1)} fusion(bf16[296,128,128]{2,1,0:T(8,128)(2,1)S(1)} %pad_maximum_fusion.2, f32[256,296]{0,1:T(8,128)S(1)} %copy-done.16), kind=kOutput, calls=%fused_computation.35 | convolution fusion | flops 7453278208 | bytes 18391040 | tf_op jit(solution)/shard_map/ic,cyz->iyz/dot_general | solution.py:44
  1049.4 24.0 %fusion.6 = f32[256,128,128]{2,1,0:T(8,128)} fusion(bf16[256,128,128]{2,0,1:T(8,128)(2,1)S(1)} %fusion.19, f32[128,128]{1,0:T(8,128)S(1)} %copy-done.13), kind=kOutput, calls=%fused_computation.22 | convolution fusion | flops 3221225472 | bytes 25231360 | tf_op jit(solution)/shard_map/xjc,xcz->xjz/dot_general | solution.py:44
  1076.2 19.2 %fusion.1 = (f32[]{:T(128)}, f32[256,128,128]{2,1,0:T(8,128)}) fusion(bf16[256,128,128]{2,1,0:T(8,128)(2,1)} %param.13, f32[256,128,128]{2,1,0:T(8,128)} %fusion.6, bf16[256,40,128]{2,0,1:T(8,128)(2,1)} %pad_maximum_fusion.10, f32[256,128,20]{1,2,0:T(8,128)} %broadcast_in_dim.157, f32[256,128,20]{1,2,0:T(8,128)S(1)} %copy-done.5), kind=kOutput, calls=%fused_computation.3 | convolution fusion | flops 1028915200 | bytes 49807364 | tf_op jit(solution)/shard_map/xjc,xcz->xjz/dot_general | solution.py:44
  1096.9 46.4 %all-reduce = f32[64]{0:T(128)S(1)} all-reduce(f32[64]{0:T(128)S(1)} %maximum_dynamic-update-slice_fusion), channel_id=2, replica_groups=mesh['gx'=4,'gy'=8] {'gx','gy'}, use_global_device_ids=true, to_apply=%add | all-reduce | flops 64 | bytes 512
  1145.3 17.0 %multiply_subtract_fusion = f32[256,128,128]{2,1,0:T(8,128)} fusion(f32[256,128,128]{2,1,0:T(8,128)} %add_subtract_fusion, f32[256,128,128]{2,1,0:T(8,128)} %get-tuple-element.169, f32[]{:T(128)} %bitcast.47), kind=kLoop, calls=%fused_computation.4 | loop fusion | flops 8388608 | bytes 50331652 | tf_op jit(solution)/shard_map/sub | solution.py:178
  1162.4 17.0 %multiply_add_fusion = f32[256,128,128]{2,1,0:T(8,128)} fusion(f32[256,128,128]{2,1,0:T(8,128)} %param.14, f32[256,128,128]{2,1,0:T(8,128)} %get-tuple-element.170, f32[]{:T(128)} %bitcast.47), kind=kLoop, calls=%fused_computation.5 | loop fusion | flops 8388608 | bytes 50331652 | tf_op jit(solution)/shard_map/add | solution.py:178
  (507 shorter events, 593.5 us)
Async XLA Ops:
  7.2 262.4 %all-gather.5.cloned.1.call-start = ((), (), s32[]{:S(2)}) async-start(), calls=%async_computation | async-start | bytes 2621440 | tf_op jit(solution)/shard_map/all_gather | solution.py:110
  7.9 273.6 %all-gather.7.cloned.1.call-start = ((), (), s32[]{:S(2)}) async-start(), calls=%async_computation.1 | async-start | bytes 2359296 | tf_op jit(solution)/shard_map/all_gather | solution.py:111
  26.6 58.8 %collective-permute-start = (bf16[20,128,128]{1,2,0:T(8,128)(2,1)}, bf16[20,128,128]{1,2,0:T(8,128)(2,1)S(1)}, u32[]{:S(2)}, u32[]{:S(2)}) collective-permute-start(bf16[20,128,128]{1,2,0:T(8,128)(2,1)} %get-tuple-element.16), channel_id=1, source_target_pairs={{0,8},{8,16},{16,24},{1,9},{9,17},{17,25},{2,10},{10,18},{18,26},{... | collective-permute-start | bytes 1966088 | tf_op jit(solution)/shard_map/ppermute | solution.py:19
  31.6 53.8 %collective-permute-start.1 = (bf16[20,128,128]{1,2,0:T(8,128)(2,1)S(1)}, bf16[20,128,128]{1,2,0:T(8,128)(2,1)S(1)}, u32[]{:S(2)}, u32[]{:S(2)}) collective-permute-start(bf16[20,128,128]{1,2,0:T(8,128)(2,1)S(1)} %get-tuple-element.17), channel_id=1, source_target_pairs={{8,0},{16,8},{24,16},{9,1},{17,9},{25,17},{10,2},{18,10},{26,18},{... | collective-permute-start | bytes 1966088 | tf_op jit(solution)/shard_map/ppermute | solution.py:22
  336.3 78.2 %collective-permute-start.50 = (bf16[8,256,128]{2,0,1:T(8,128)(2,1)S(1)}, bf16[8,256,128]{2,0,1:T(8,128)(2,1)S(1)}, u32[]{:S(2)}, u32[]{:S(2)}) collective-permute-start(bf16[8,256,128]{2,0,1:T(8,128)(2,1)S(1)} %get-tuple-element.63), channel_id=1, source_target_pairs={{0,24},{8,0},{16,8},{24,16},{1,25},{9,1},{17,9},{25,17},{2,26},{10... | collective-permute-start | bytes 1572872 | tf_op jit(solution)/shard_map/ppermute | solution.py:64
  340.1 104.3 %collective-permute-start.49 = (bf16[8,256,128]{2,0,1:T(8,128)(2,1)S(1)}, bf16[8,256,128]{2,0,1:T(8,128)(2,1)S(1)}, u32[]{:S(2)}, u32[]{:S(2)}) collective-permute-start(bf16[8,256,128]{2,0,1:T(8,128)(2,1)S(1)} %get-tuple-element.64), channel_id=1, source_target_pairs={{0,16},{8,24},{16,0},{24,8},{1,17},{9,25},{17,1},{25,9},{2,18},{10... | collective-permute-start | bytes 1572872 | tf_op jit(solution)/shard_map/ppermute | solution.py:64
  341.7 102.6 %collective-permute-start.48 = (bf16[8,256,128]{2,0,1:T(8,128)(2,1)S(1)}, bf16[8,256,128]{2,0,1:T(8,128)(2,1)S(1)}, u32[]{:S(2)}, u32[]{:S(2)}) collective-permute-start(bf16[8,256,128]{2,0,1:T(8,128)(2,1)S(1)} %get-tuple-element.65), channel_id=1, source_target_pairs={{0,8},{8,16},{16,24},{24,0},{1,9},{9,17},{17,25},{25,1},{2,10},{10... | collective-permute-start | bytes 1572872 | tf_op jit(solution)/shard_map/ppermute | solution.py:64
  377.7 79.7 %collective-permute-start.30 = (bf16[8,256,128]{2,0,1:T(8,128)(2,1)S(1)}, bf16[8,256,128]{2,0,1:T(8,128)(2,1)S(1)}, u32[]{:S(2)}, u32[]{:S(2)}) collective-permute-start(bf16[8,256,128]{2,0,1:T(8,128)(2,1)S(1)} %get-tuple-element.87), channel_id=1, source_target_pairs={{0,24},{8,0},{16,8},{24,16},{1,25},{9,1},{17,9},{25,17},{2,26},{10... | collective-permute-start | bytes 1572872 | tf_op jit(solution)/shard_map/ppermute | solution.py:64
  377.9 111.3 %collective-permute-start.29 = (bf16[8,256,128]{2,0,1:T(8,128)(2,1)S(1)}, bf16[8,256,128]{2,0,1:T(8,128)(2,1)S(1)}, u32[]{:S(2)}, u32[]{:S(2)}) collective-permute-start(bf16[8,256,128]{2,0,1:T(8,128)(2,1)S(1)} %get-tuple-element.88), channel_id=1, source_target_pairs={{0,16},{8,24},{16,0},{24,8},{1,17},{9,25},{17,1},{25,9},{2,18},{10... | collective-permute-start | bytes 1572872 | tf_op jit(solution)/shard_map/ppermute | solution.py:64
  414.5 82.8 %collective-permute-start.28 = (bf16[8,256,128]{2,0,1:T(8,128)(2,1)S(1)}, bf16[8,256,128]{2,0,1:T(8,128)(2,1)S(1)}, u32[]{:S(2)}, u32[]{:S(2)}) collective-permute-start(bf16[8,256,128]{2,0,1:T(8,128)(2,1)S(1)} %get-tuple-element.89), channel_id=1, source_target_pairs={{0,8},{8,16},{16,24},{24,0},{1,9},{9,17},{17,25},{25,1},{2,10},{10... | collective-permute-start | bytes 1572872 | tf_op jit(solution)/shard_map/ppermute | solution.py:64
  444.3 60.0 %collective-permute-start.10 = (bf16[8,256,128]{2,0,1:T(8,128)(2,1)S(1)}, bf16[8,256,128]{2,0,1:T(8,128)(2,1)S(1)}, u32[]{:S(2)}, u32[]{:S(2)}) collective-permute-start(bf16[8,256,128]{2,0,1:T(8,128)(2,1)S(1)} %get-tuple-element.130), channel_id=1, source_target_pairs={{0,24},{8,0},{16,8},{24,16},{1,25},{9,1},{17,9},{25,17},{2,26},{10... | collective-permute-start | bytes 1572872 | tf_op jit(solution)/shard_map/ppermute | solution.py:64
  444.3 67.4 %collective-permute-start.9 = (bf16[8,256,128]{2,0,1:T(8,128)(2,1)S(1)}, bf16[8,256,128]{2,0,1:T(8,128)(2,1)S(1)}, u32[]{:S(2)}, u32[]{:S(2)}) collective-permute-start(bf16[8,256,128]{2,0,1:T(8,128)(2,1)S(1)} %get-tuple-element.131), channel_id=1, source_target_pairs={{0,16},{8,24},{16,0},{24,8},{1,17},{9,25},{17,1},{25,9},{2,18},{10... | collective-permute-start | bytes 1572872 | tf_op jit(solution)/shard_map/ppermute | solution.py:64
  457.4 65.9 %collective-permute-start.8 = (bf16[8,256,128]{2,0,1:T(8,128)(2,1)S(1)}, bf16[8,256,128]{2,0,1:T(8,128)(2,1)S(1)}, u32[]{:S(2)}, u32[]{:S(2)}) collective-permute-start(bf16[8,256,128]{2,0,1:T(8,128)(2,1)S(1)} %get-tuple-element.132), channel_id=1, source_target_pairs={{0,8},{8,16},{16,24},{24,0},{1,9},{9,17},{17,25},{25,1},{2,10},{10... | collective-permute-start | bytes 1572872 | tf_op jit(solution)/shard_map/ppermute | solution.py:64
  489.3 60.3 %collective-permute-start.77 = (bf16[8,128,128]{1,2,0:T(8,128)(2,1)S(1)}, bf16[8,128,128]{1,2,0:T(8,128)(2,1)S(1)}, u32[]{:S(2)}, u32[]{:S(2)}) collective-permute-start(bf16[8,128,128]{1,2,0:T(8,128)(2,1)S(1)} %get-tuple-element.30), channel_id=1, source_target_pairs={{0,7},{1,0},{2,1},{3,2},{4,3},{5,4},{6,5},{7,6},{8,15},{9,8},{10,9... | collective-permute-start | bytes 786440 | tf_op jit(solution)/shard_map/ppermute | solution.py:64
  497.3 51.9 %collective-permute-start.76 = (bf16[8,128,128]{1,2,0:T(8,128)(2,1)S(1)}, bf16[8,128,128]{1,2,0:T(8,128)(2,1)S(1)}, u32[]{:S(2)}, u32[]{:S(2)}) collective-permute-start(bf16[8,128,128]{1,2,0:T(8,128)(2,1)S(1)} %get-tuple-element.31), channel_id=1, source_target_pairs={{0,6},{1,7},{2,0},{3,1},{4,2},{5,3},{6,4},{7,5},{8,14},{9,15},{10,... | collective-permute-start | bytes 786440 | tf_op jit(solution)/shard_map/ppermute | solution.py:64
  532.9 56.2 %collective-permute-start.57 = (bf16[8,128,128]{1,2,0:T(8,128)(2,1)S(1)}, bf16[8,128,128]{1,2,0:T(8,128)(2,1)}, u32[]{:S(2)}, u32[]{:S(2)}) collective-permute-start(bf16[8,128,128]{1,2,0:T(8,128)(2,1)S(1)} %get-tuple-element.54), channel_id=1, source_target_pairs={{0,7},{1,0},{2,1},{3,2},{4,3},{5,4},{6,5},{7,6},{8,15},{9,8},{10,9... | collective-permute-start | bytes 786440 | tf_op jit(solution)/shard_map/ppermute | solution.py:64
  569.2 52.5 %collective-permute-start.17 = (bf16[8,128,128]{1,2,0:T(8,128)(2,1)}, bf16[8,128,128]{1,2,0:T(8,128)(2,1)}, u32[]{:S(2)}, u32[]{:S(2)}) collective-permute-start(bf16[8,128,128]{1,2,0:T(8,128)(2,1)} %get-tuple-element.121), channel_id=1, source_target_pairs={{0,7},{1,0},{2,1},{3,2},{4,3},{5,4},{6,5},{7,6},{8,15},{9,8},{10,9... | collective-permute-start | bytes 786440 | tf_op jit(solution)/shard_map/ppermute | solution.py:64
  606.5 55.4 %collective-permute-start.37 = (bf16[8,128,128]{1,2,0:T(8,128)(2,1)}, bf16[8,128,128]{1,2,0:T(8,128)(2,1)}, u32[]{:S(2)}, u32[]{:S(2)}) collective-permute-start(bf16[8,128,128]{1,2,0:T(8,128)(2,1)} %get-tuple-element.78), channel_id=1, source_target_pairs={{0,7},{1,0},{2,1},{3,2},{4,3},{5,4},{6,5},{7,6},{8,15},{9,8},{10,9... | collective-permute-start | bytes 786440 | tf_op jit(solution)/shard_map/ppermute | solution.py:64
  642.8 129.6 %collective-permute-start.79 = (bf16[8,128,128]{2,1,0:T(8,128)(2,1)}, bf16[8,128,128]{2,1,0:T(8,128)(2,1)}, u32[]{:S(2)}, u32[]{:S(2)}) collective-permute-start(bf16[8,128,128]{2,1,0:T(8,128)(2,1)} %get-tuple-element.27), channel_id=1, source_target_pairs={{0,2},{1,3},{2,4},{3,5},{4,6},{5,7},{6,0},{7,1},{8,10},{9,11},{10,... | collective-permute-start | bytes 786440 | tf_op jit(solution)/shard_map/ppermute | solution.py:64
  644.5 115.5 %collective-permute-start.78 = (bf16[8,128,128]{2,1,0:T(8,128)(2,1)}, bf16[8,128,128]{2,1,0:T(8,128)(2,1)}, u32[]{:S(2)}, u32[]{:S(2)}) collective-permute-start(bf16[8,128,128]{2,1,0:T(8,128)(2,1)} %get-tuple-element.28), channel_id=1, source_target_pairs={{0,1},{1,2},{2,3},{3,4},{4,5},{5,6},{6,7},{7,0},{8,9},{9,10},{10,1... | collective-permute-start | bytes 786440 | tf_op jit(solution)/shard_map/ppermute | solution.py:64
  750.5 52.5 %collective-permute-start.27 = (bf16[8,256,128]{1,2,0:T(8,128)(2,1)S(1)}, bf16[8,256,128]{1,2,0:T(8,128)(2,1)S(1)}, u32[]{:S(2)}, u32[]{:S(2)}) collective-permute-start(bf16[8,256,128]{1,2,0:T(8,128)(2,1)S(1)} %get-tuple-element.90), channel_id=1, source_target_pairs={{0,24},{8,0},{16,8},{24,16},{1,25},{9,1},{17,9},{25,17},{2,26},{10... | collective-permute-start | bytes 1572872 | tf_op jit(solution)/shard_map/ppermute | solution.py:64
  760.1 66.2 %collective-permute-start.84 = (bf16[8,128,128]{2,1,0:T(8,128)(2,1)S(1)}, bf16[8,128,128]{2,1,0:T(8,128)(2,1)S(1)}, u32[]{:S(2)}, u32[]{:S(2)}) collective-permute-start(bf16[8,128,128]{2,1,0:T(8,128)(2,1)S(1)} %get-tuple-element.22), channel_id=1, source_target_pairs={{0,7},{1,0},{2,1},{3,2},{4,3},{5,4},{6,5},{7,6},{8,15},{9,8},{10,9... | collective-permute-start | bytes 786440 | tf_op jit(solution)/shard_map/ppermute | solution.py:64
  772.4 53.8 %collective-permute-start.83 = (bf16[8,128,128]{2,1,0:T(8,128)(2,1)S(1)}, bf16[8,128,128]{2,1,0:T(8,128)(2,1)S(1)}, u32[]{:S(2)}, u32[]{:S(2)}) collective-permute-start(bf16[8,128,128]{2,1,0:T(8,128)(2,1)S(1)} %get-tuple-element.23), channel_id=1, source_target_pairs={{0,6},{1,7},{2,0},{3,1},{4,2},{5,3},{6,4},{7,5},{8,14},{9,15},{10,... | collective-permute-start | bytes 786440 | tf_op jit(solution)/shard_map/ppermute | solution.py:64
  858.8 58.7 %collective-permute-start.67 = (bf16[8,256,128]{1,2,0:T(8,128)(2,1)S(1)}, bf16[8,256,128]{1,2,0:T(8,128)(2,1)S(1)}, u32[]{:S(2)}, u32[]{:S(2)}) collective-permute-start(bf16[8,256,128]{1,2,0:T(8,128)(2,1)S(1)} %get-tuple-element.42), channel_id=1, source_target_pairs={{0,24},{8,0},{16,8},{24,16},{1,25},{9,1},{17,9},{25,17},{2,26},{10... | collective-permute-start | bytes 1572872 | tf_op jit(solution)/shard_map/ppermute | solution.py:64
  (134 other events, 2307.1 us)
Sparse Core Ops, SparseCore 0:
  9.6 59.0 all-gather.4
  70.6 30.1 all-gather.6
